TPU v7x, 128 devices: a whole 4x4x4 slice. The times are simulated.
128 devices in a mesh: seq: 32 (over z_hi, y, x), kv: 4 (over z_lo, core).
Axes of the slice: x: 4, y: 4, z: 4 (z_hi: 2, z_lo: 2; z = z_hi * 2 + z_lo), core: 2. Of those that a mesh axis runs over, the one named last changes fastest.
Arguments:
- queries: bfloat16 [8192, 3584], P('seq', 'kv'), may hold values from -36 to 36
- keys: bfloat16 [8192, 512], P('seq', 'kv'), may hold values from -6 to 6
- values: bfloat16 [8192, 512], P('seq', 'kv'), may hold values from -6 to 6
- doc_lengths: int32 [16], replicated, may hold values from 1 to 68, 128 in all
- out_weight: bfloat16 [3584, 3584], P(None, 'kv'), may hold values from -0.796875 to 0.796875
Outputs:
- mixed: bfloat16 [8192, 3584], P('seq', 'kv')
Inputs may be any that keep to these rules, and one draw needn't show every extreme that they name: `doc_lengths`: the lengths sum to 128 and the largest is exactly 68.
All inputs are finite; a program needn't handle non-finite values.
Results may differ from a plain program's by a relative error of at most 0.009.
Values may be sent and summed in bfloat16 or wider, within the bound.
No kernel may reach another device: no remote copies, remote signals or barrier semaphores. Data moves between devices by JAX's collectives and lax.ppermute only.
A program may use at most 64 MiB of HBM per device.

v0:
```python
import math

import jax
import jax.numpy as jnp
from jax import lax
from jax.sharding import PartitionSpec as P

HD = 128
GRAIN = 64


masked_score = -1e30


def document_of(positions, doc_ends):
    return jnp.sum((doc_ends[None, :] <= positions[:, None]).astype(jnp.int32), axis=1)


def attend_block(state, query_heads, query_doc, key_block, value_block, key_start, doc_ends):
    peak_old, total_old, summed_old = state
    key_count = key_block.shape[0]
    local_heads = query_heads.shape[1]
    key_doc = document_of(key_start + jnp.arange(key_count, dtype=jnp.int32), doc_ends)
    key_heads = key_block.reshape(key_count, local_heads, HD)
    value_heads = value_block.reshape(key_count, local_heads, HD)
    scores = jnp.einsum(
        "qkgd,tkd->kgqt", query_heads, key_heads, preferred_element_type=jnp.float32
    )
    scores = scores * (1.0 / HD**0.5)
    allowed = (query_doc[:, None] == key_doc[None, :])[None, None]
    masked = jnp.where(allowed, scores, masked_score)
    peak_new = jnp.maximum(peak_old, jnp.max(masked, axis=-1))
    expo = jnp.where(allowed, jnp.exp(masked - peak_new[..., None]), 0.0)
    shrink = jnp.exp(peak_old - peak_new)
    total_new = total_old * shrink + jnp.sum(expo, axis=-1)
    summed_new = summed_old * shrink[..., None] + jnp.einsum(
        "kgqt,tkd->kgqd", expo.astype(jnp.bfloat16), value_heads, preferred_element_type=jnp.float32
    )
    return (peak_new, total_new, summed_new)


def maybe_attend(state, query_heads, query_doc, key_block, value_block, key_start, doc_ends):
    key_count = key_block.shape[0]
    total_tokens = doc_ends[-1]
    inside = (key_start >= 0) & (key_start < total_tokens)
    first_doc = document_of(jnp.reshape(key_start, (1,)), doc_ends)[0]
    last_doc = document_of(jnp.reshape(key_start + key_count - 1, (1,)), doc_ends)[0]
    needed = inside & (first_doc <= query_doc[-1]) & (last_doc >= query_doc[0])

    def work(current):
        return attend_block(
            current, query_heads, query_doc, key_block, value_block, key_start, doc_ends
        )

    def keep(current):
        return current

    return lax.cond(needed, work, keep, state)


def per_device(queries, keys, values, doc_lengths, out_weight):
    q_rows = queries.shape[0]
    local_heads = keys.shape[1] // HD
    per_group = queries.shape[1] // keys.shape[1]
    doc_ends = jnp.cumsum(doc_lengths) * GRAIN
    my_index = lax.axis_index("seq")
    query_doc = document_of(my_index * q_rows + jnp.arange(q_rows, dtype=jnp.int32), doc_ends)
    query_heads = queries.reshape(q_rows, local_heads, per_group, HD)
    initial = (
        jnp.full((local_heads, per_group, q_rows), masked_score, jnp.float32),
        jnp.zeros((local_heads, per_group, q_rows), jnp.float32),
        jnp.zeros((local_heads, per_group, q_rows, HD), jnp.float32),
    )
    key_piece = lax.all_gather(keys, "seq", axis=0, tiled=True)
    value_piece = lax.all_gather(values, "seq", axis=0, tiled=True)
    piece_rows = key_piece.shape[0]
    block_rows = math.gcd(piece_rows, q_rows)

    def advance(block_index, current):
        offset = (block_index * block_rows).astype(jnp.int32)
        key_block = lax.dynamic_slice_in_dim(key_piece, offset, block_rows, 0)
        value_block = lax.dynamic_slice_in_dim(value_piece, offset, block_rows, 0)
        return maybe_attend(
            current, query_heads, query_doc, key_block, value_block, offset, doc_ends
        )

    state = lax.fori_loop(0, piece_rows // block_rows, advance, initial)
    peak_final, total_final, summed_final = state
    result = summed_final / total_final[..., None]
    attended = jnp.transpose(result, (2, 0, 1, 3)).reshape(q_rows, local_heads * per_group * HD)
    attended = attended.astype(jnp.bfloat16)
    mixed = jnp.dot(
        lax.all_gather(attended, "kv", axis=1, tiled=True),
        out_weight,
        preferred_element_type=jnp.float32,
    )
    return mixed.astype(jnp.bfloat16)


def solution(mesh):
    return jax.shard_map(
        per_device,
        mesh=mesh,
        in_specs=(P("seq", "kv"), P("seq", "kv"), P("seq", "kv"), P(), P(None, "kv")),
        out_specs=P("seq", "kv"),
        check_vma=False,
    )
```

profile of v0, /device:TPU:25, one launch (start us, length us, event | category | flops | bytes accessed | tf_op | source)
XLA Modules:
  0.0 429.0 jit_solution(5514056437500515322)
XLA Ops:
  8.1 0.7 copy.14
  8.8 1.2 copy.15
  10.5 71.2 %all-gather.4.cloned.1.call-done = bf16[8192,128]{1,0:T(8,128)(2,1)} async-done(((bf16[256,128]{1,0:T(8,128)(2,1)}), bf16[8192,128]{1,0:T(8,128)(2,1)}) %all-gather.4.cloned.1.call-update) | async-done | bytes 2097168 | tf_op jit(solution)/shard_map/all_gather | solution.py:74
  81.7 72.1 %all-gather.6.cloned.1.call-done = bf16[8192,128]{1,0:T(8,128)(2,1)} async-done(((bf16[256,128]{1,0:T(8,128)(2,1)}), bf16[8192,128]{1,0:T(8,128)(2,1)}) %all-gather.6.cloned.1.call-update) | async-done | bytes 2097168 | tf_op jit(solution)/shard_map/all_gather | solution.py:75
  153.8 229.2 %while.21 = (s32[]{:T(128)}, f32[1,7,256]{2,1,0:T(8,128)S(1)}, f32[1,7,256]{2,1,0:T(8,128)S(1)}, f32[1,7,256,128]{3,2,1,0:T(8,128)S(1)}, s32[16]{0:T(128)S(1)}, ...) while((s32[]{:T(128)}, f32[1,7,256]{2,1,0:T(8,128)S(1)}, ...), condition=%wide.region_10.11_spmd, body=%wide.region_2.10_spmd.sunk | while | flops 241386864 | bytes 8312349 | solution.py:87
  155.1 0.7 fusion.30
  160.1 0.7 fusion.30
  183.7 3.9 conditional.2
  184.0 1.3 fusion
  185.3 1.8 fusion.3
  192.6 3.9 conditional.2
  192.8 1.3 fusion
  194.2 1.8 fusion.3
  201.5 3.9 conditional.2
  201.7 1.3 fusion
  203.0 1.8 fusion.3
  210.3 3.9 conditional.2
  210.6 1.3 fusion
  211.9 1.8 fusion.3
  219.2 3.9 conditional.2
  219.4 1.3 fusion
  220.7 1.8 fusion.3
  228.0 3.9 conditional.2
  228.3 1.3 fusion
  229.6 1.8 fusion.3
  236.9 3.9 conditional.2
  237.1 1.3 fusion
  238.4 1.8 fusion.3
  245.7 3.9 conditional.2
  246.0 1.3 fusion
  247.3 1.8 fusion.3
  254.6 3.9 conditional.2
  254.8 1.3 fusion
  256.1 1.8 fusion.3
  263.4 3.9 conditional.2
  263.7 1.3 fusion
  265.0 1.8 fusion.3
  272.3 3.9 conditional.2
  272.5 1.3 fusion
  273.8 1.8 fusion.3
  281.1 3.9 conditional.2
  281.4 1.3 fusion
  282.7 1.8 fusion.3
  290.0 3.9 conditional.2
  290.2 1.3 fusion
  291.5 1.8 fusion.3
  298.8 3.9 conditional.2
  299.1 1.3 fusion
  300.4 1.8 fusion.3
  307.7 3.9 conditional.2
  307.9 1.3 fusion
  309.2 1.8 fusion.3
  316.5 3.9 conditional.2
  316.8 1.3 fusion
  318.1 1.8 fusion.3
  325.4 3.9 conditional.2
  325.6 1.3 fusion
  326.9 1.8 fusion.3
  334.2 3.9 conditional.2
  334.5 1.3 fusion
  335.8 1.8 fusion.3
  383.3 0.9 divide_convert_fusion
  384.2 32.0 %all-gather.8.cloned.1.call-done = bf16[256,3584]{0,1:T(8,128)(2,1)} async-done(((bf16[256,896]{0,1:T(8,128)(2,1)}), bf16[256,3584]{0,1:T(8,128)(2,1)}) %all-gather.8.cloned.1.call-update) | async-done | bytes 1835024 | tf_op jit(solution)/shard_map/all_gather | solution.py:93
  416.2 6.3 %convolution_convert_fusion = bf16[256,896]{1,0:T(8,128)(2,1)} fusion(bf16[256,3584]{0,1:T(8,128)(2,1)} %all-gather.8.cloned.1.call-done, bf16[3584,896]{1,0:T(8,128)(2,1)} %param.13), kind=kOutput, calls=%fused_computation.35 | convolution fusion | flops 1644396544 | bytes 8716288 | tf_op jit(solution)/shard_map/dot_general | solution.py:92
  (249 shorter events, 73.9 us)
Async XLA Ops:
  6.5 75.2 %all-gather.4.cloned.1.call-start = ((), (), s32[]{:S(2)}) async-start(), calls=%async_computation | async-start | bytes 2162688 | tf_op jit(solution)/shard_map/all_gather | solution.py:74
  7.3 146.5 %all-gather.6.cloned.1.call-start = ((), (), s32[]{:S(2)}) async-start(), calls=%async_computation.1 | async-start | bytes 2162688 | tf_op jit(solution)/shard_map/all_gather | solution.py:75
  8.0 408.2 %all-gather.8.cloned.1.call-start = ((), (), s32[]{:S(2)}) async-start(), calls=%async_computation.2 | async-start | bytes 2293760 | tf_op jit(solution)/shard_map/all_gather | solution.py:93
Sparse Core Ops, SparseCore 0:
  10.4 71.2 all-gather.3
  84.8 68.9 all-gather.5
  384.3 31.8 all-gather.7
where the time goes:
time: 433 us; the launch traced here: 429 us
  waiting for transfers between devices  177 us (41%)
  loops' own time  100 us (23%)
  matrix products  62.4 us (14%)
  local copies, waits for them, and re-layouts  40.6 us (9%)
  other arithmetic  35.9 us (8%)
  between operations  13.2 us (3%)
    another operation x1, loops' own time, per_device(): state = lax.fori_loop(0, piece_rows // block_rows, advance, initial)  98.6 us
    all_gather x1, waiting for transfers between devices, per_device(): value_piece = lax.all_gather(values, 'seq', axis=0, tiled=True)  72.1 us
    all_gather x1, waiting for transfers between devices, per_device(): key_piece = lax.all_gather(keys, 'seq', axis=0, tiled=True)  71.2 us
    dot_general x18, matrix products, attend_block(): jnp.einsum('kgqt,tkd->kgqd', expo.astype(jnp.bfloat16), value_heads, pref...  33 us
    all_gather x1, waiting for transfers between devices, per_device(): lax.all_gather(attended, 'kv', axis=1, tiled=True)  32 us
    reduce_sum x51, other arithmetic, document_of(): jnp.sum((doc_ends[None, :] <= positions[:, None]).astype(jnp.int32), axis=1)  24.4 us
    dot_general x18, matrix products, attend_block(): jnp.einsum('qkgd,tkd->kgqt', query_heads, key_heads, preferred_element_ty...  23.2 us
    slice x32, local copies, waits for them, and re-layouts, maybe_attend(): total_tokens = doc_ends[-1]  19.6 us
  transfers between devices with their start and end apart: 3, of which 3 were waited for; matrix products, arithmetic and copies ran while one was open for 1% of the time, Pallas kernels for 0%

commit v1 on v0

v1 whole, which is shorter than its diff:
```python
import jax
import jax.numpy as jnp
import numpy as np
from jax import lax
from jax.experimental import pallas as pl
from jax.experimental.pallas import tpu as pltpu
from jax.sharding import Mesh, PartitionSpec as P

HD = 128
GRAIN = 64
TOK = 256
HEADS = 7
SEQ = 8192
DOCS = 16
LONG = 4352
LONG_GRAINS = LONG // GRAIN
GRAINS = TOK // GRAIN
ROWS = HEADS * GRAIN
HALF = LONG // 2
SMALL = 256
SCALE = 1.4426950408889634 / HD**0.5
LOWEST = -1e30
PLANE = ("y", "x", "c")
OFFSETS = (0, -1, 1, 2)


def turn(by_first, by_second):
    pairs = []
    for y in range(4):
        for x in range(4):
            pairs.append((y, x, 0, (y + by_first) % 4, (x + by_second) % 4))
            pairs.append((y, x, 1, (y + by_second) % 4, (x + by_first) % 4))
    return [((y * 4 + x) * 2 + c, (to_y * 4 + to_x) * 2 + c) for y, x, c, to_y, to_x in pairs]


def swap(block, axis):
    return lax.ppermute(block, axis, [(0, 1), (1, 0)])


def softmax_step(state, query, keys, values, allowed):
    peak, summed = state
    scores = lax.dot_general(
        query, keys, (((1,), (1,)), ((), ())), preferred_element_type=jnp.float32
    )
    scores = scores * SCALE
    if allowed is not None:
        scores = jnp.where(allowed, scores, LOWEST)
    peak_new = jnp.maximum(peak, jnp.max(scores, axis=1, keepdims=True))
    weights = jnp.exp2(scores - peak_new).astype(jnp.bfloat16)
    product = jnp.dot(weights, values, preferred_element_type=jnp.float32)
    return peak_new, summed * jnp.exp2(peak - peak_new) + product


def attend_kernel(lengths, place, queries, b0, b1, b2, b3, out, keys, values, sems, rows, result):
    zh, y, x, c = place[0], place[1], place[2], place[3]
    copies = []
    for outer, (ref, far) in enumerate(zip((b0, b1, b2, b3), OFFSETS)):
        for inner, near in enumerate(OFFSETS):
            up = jnp.where(c == 0, far, near)
            across = jnp.where(c == 0, near, far)
            for other in range(2):
                plane = zh ^ other
                at = plane * 16 + ((y + up + 4) % 4) * 4 + (x + across + 4) % 4
                at = pl.multiple_of(at * TOK, TOK)
                src = pl.ds((inner * 2 + other) * TOK, TOK)
                copies.append(pltpu.make_async_copy(
                    ref.at[src, pl.ds(0, HD)], keys.at[pl.ds(at, TOK), :], sems.at[0, outer * 8 + inner * 2 + other]))
                copies.append(pltpu.make_async_copy(
                    ref.at[src, pl.ds(HD, HD)], values.at[pl.ds(at, TOK), pl.ds(0, HD)], sems.at[1, outer * 8 + inner * 2 + other]))
    for copy in copies:
        copy.start()
    values[:, HD:] = jnp.ones((SEQ + SMALL, HD), jnp.bfloat16)
    values[SEQ:, :HD] = jnp.zeros((SMALL, HD), jnp.bfloat16)
    for grain in range(GRAINS):
        for head in range(HEADS):
            rows[pl.ds(grain * ROWS + head * GRAIN, GRAIN), :] = queries[
                pl.ds(grain * GRAIN, GRAIN), pl.ds(head * HD, HD)]
    for copy in copies:
        copy.wait()

    first_grain = ((zh * 4 + y) * 4 + x) * GRAINS

    def one_grain(grain, carry):
        at = first_grain + grain
        begin, end, total = jnp.int32(0), jnp.int32(0), jnp.int32(0)
        for doc in range(DOCS):
            after = total + lengths[doc]
            here = (total <= at) & (at < after)
            begin = jnp.where(here, total, begin)
            end = jnp.where(here, after, end)
            total = after
        span = pl.ds(pl.multiple_of(grain * ROWS, ROWS), ROWS)
        is_long = end - begin == LONG_GRAINS
        initial = (jnp.full((ROWS, 1), LOWEST, jnp.float32), jnp.zeros((ROWS, 2 * HD), jnp.float32))

        def finish(summed):
            result[...] = (summed[:, :HD] / summed[:, HD:]).astype(jnp.bfloat16)
            for head in range(HEADS):
                out[pl.ds(pl.multiple_of(grain * GRAIN, GRAIN), GRAIN), pl.ds(head * HD, HD)] = result[
                    pl.ds(head * GRAIN, GRAIN), :]

        @pl.when(is_long)
        def _():
            query, state = rows[span, :], initial
            for half in range(2):
                part = pl.ds(pl.multiple_of(begin * GRAIN + half * HALF, GRAIN), HALF)
                state = softmax_step(state, query, keys[part, :], values[part, :], None)
            finish(state[1])

        @pl.when(jnp.logical_not(is_long))
        def _():
            query = rows[span, :]
            column = lax.broadcasted_iota(jnp.int32, (1, SMALL), 1)

            def step(index, state):
                start = begin * GRAIN + index * SMALL
                part = pl.ds(pl.multiple_of(start, GRAIN), SMALL)
                return softmax_step(
                    state, query, keys[part, :], values[part, :], column < end * GRAIN - start)

            steps = ((end - begin) * GRAIN + SMALL - 1) // SMALL
            finish(lax.fori_loop(0, steps, step, initial)[1])

        return carry

    lax.fori_loop(0, GRAINS, one_grain, 0)


def attend(lengths, place, queries, blocks):
    smem = pl.BlockSpec(memory_space=pltpu.SMEM)
    vmem = pl.BlockSpec(memory_space=pltpu.VMEM)
    hbm = pl.BlockSpec(memory_space=pl.ANY)
    return pl.pallas_call(
        attend_kernel,
        out_shape=jax.ShapeDtypeStruct((TOK, HEADS * HD), jnp.bfloat16),
        in_specs=[smem, smem, vmem] + [hbm] * 4,
        out_specs=vmem,
        scratch_shapes=[
            pltpu.VMEM((SEQ + SMALL, HD), jnp.bfloat16),
            pltpu.VMEM((SEQ + SMALL, 2 * HD), jnp.bfloat16),
            pltpu.SemaphoreType.DMA((2, 32)),
            pltpu.VMEM((GRAINS * ROWS, HD), jnp.bfloat16),
            pltpu.VMEM((ROWS, HD), jnp.bfloat16),
        ],
        compiler_params=pltpu.CompilerParams(vmem_limit_bytes=48 * 2**20),
    )(lengths, place, queries, *blocks)


def per_device(queries, keys, values, doc_lengths, out_weight):
    zh, y, x, zl, c = (lax.axis_index(a) for a in ("zh", "y", "x", "zl", "c"))
    own = jnp.concatenate([keys, values], axis=1)
    pair = jnp.concatenate([own, swap(own, "zh")], axis=0)
    near = jnp.concatenate(
        [pair] + [lax.ppermute(pair, PLANE, turn(0, -k)) for k in OFFSETS[1:]], axis=0
    )
    blocks = [near] + [lax.ppermute(near, PLANE, turn(-k, 0)) for k in OFFSETS[1:]]
    place = jnp.stack([zh, y, x, c]).astype(jnp.int32)
    attended = attend(doc_lengths, place, queries, blocks)
    across = swap(attended, "zl")
    parts = [attended, swap(attended, "c"), across, swap(across, "c")]
    group = zl * 2 + c
    weight = out_weight.reshape(4, HEADS * HD, out_weight.shape[1])
    mixed = 0.0
    for index, part in enumerate(parts):
        mixed = mixed + jnp.dot(
            part,
            lax.dynamic_index_in_dim(weight, group ^ index, 0, keepdims=False),
            preferred_element_type=jnp.float32,
        )
    return mixed.astype(jnp.bfloat16)


def solution(mesh):
    fine = Mesh(np.asarray(mesh.devices).reshape(2, 4, 4, 2, 2), ("zh", "y", "x", "zl", "c"))
    seq, kv = ("zh", "y", "x"), ("zl", "c")
    return jax.shard_map(
        per_device,
        mesh=fine,
        in_specs=(P(seq, kv), P(seq, kv), P(seq, kv), P(), P(None, kv)),
        out_specs=P(seq, kv),
        check_vma=False,
    )
```

time: 433 us -> 85.4 us (0.20)
  waiting for transfers between devices: 177 us -> 38.4 us
  loops' own time: 100 us -> 0 us
  matrix products: 62.4 us -> 9.23 us
  local copies, waits for them, and re-layouts: 40.6 us -> 3.48 us
  other arithmetic: 35.9 us -> 0.09 us
  starting transfers between devices: 0.08 us -> 18.7 us
  Pallas kernels: 0 us -> 14.8 us
  between operations: 13.2 us -> 0.1 us
    all_gather x3 -> x0, waiting for transfers between devices: 175 us -> none  [the longest x1 72.1 us: per_device(): value_piece = lax.all_gather(values, 'seq', axis=0, tiled=True)]
    another operation x33 -> x0, loops' own time: 100 us -> none  [the longest x1 98.6 us: per_device(): state = lax.fori_loop(0, piece_rows // block_rows, advance, initial)]
    dot_general x37 -> x4, matrix products: 62.4 us -> 9.23 us  [per_device(): jnp.dot(part, lax.dynamic_index_in_dim(weight, group ^ index, 0, keepdims...]
    ppermute x0 -> x10, waiting for transfers between devices: none -> 38.4 us  [the longest x3 23.3 us: per_device(): lax.ppermute(near, PLANE, turn(-k, 0))]
    slice x64 -> x0, local copies, waits for them, and re-layouts: 37.9 us -> none  [the longest x32 19.6 us: maybe_attend(): total_tokens = doc_ends[-1]]
    reduce_sum x69 -> x0, other arithmetic: 32.5 us -> none  [the longest x51 24.4 us: document_of(): jnp.sum((doc_ends[None, :] <= positions[:, None]).astype(jnp.int32), axis=1)]
    ppermute x0 -> x10, starting transfers between devices: none -> 18.7 us  [the longest x4 12.1 us: swap(): return lax.ppermute(block, axis, [(0, 1), (1, 0)])]
    pallas_call x0 -> x1, Pallas kernels: none -> 14.8 us  [attend(): pl.pallas_call(attend_kernel, out_shape=jax.ShapeDtypeStruct((TOK, HEADS...]
  transfers between devices with their start and end apart: 3 -> 10, of which waited for: 3 -> 7; matrix products, arithmetic and copies ran while one was open for 1% -> 8% of each run, Pallas kernels for 0% -> 0%
where the time goes in v1:
time: 85.4 us; the launch traced here: 84.7 us
  waiting for transfers between devices  38.4 us (45%)
  starting transfers between devices  18.7 us (22%)
  Pallas kernels  14.8 us (17%)
  matrix products  9.23 us (11%)
  local copies, waits for them, and re-layouts  3.48 us (4%)
    ppermute x3, waiting for transfers between devices, per_device(): lax.ppermute(near, PLANE, turn(-k, 0))  23.3 us
    pallas_call x1, Pallas kernels, attend(): pl.pallas_call(attend_kernel, out_shape=jax.ShapeDtypeStruct((TOK, HEADS...  14.8 us
    ppermute x4, starting transfers between devices, swap(): return lax.ppermute(block, axis, [(0, 1), (1, 0)])  12.1 us
    dot_general x4, matrix products, per_device(): jnp.dot(part, lax.dynamic_index_in_dim(weight, group ^ index, 0, keepdims...  9.23 us
    ppermute x4, waiting for transfers between devices, swap(): return lax.ppermute(block, axis, [(0, 1), (1, 0)])  7.86 us
    ppermute x3, waiting for transfers between devices, per_device(): lax.ppermute(pair, PLANE, turn(0, -k))  7.17 us
    ppermute x3, starting transfers between devices, per_device(): lax.ppermute(near, PLANE, turn(-k, 0))  4.12 us
    unnamed x8, local copies, waits for them, and re-layouts  2.57 us
  transfers between devices with their start and end apart: 10, of which 7 were waited for; matrix products, arithmetic and copies ran while one was open for 8% of the time, Pallas kernels for 0%

profile of v1, /device:TPU:25, one launch (start us, length us, event | category | flops | bytes accessed | tf_op | source)
XLA Modules:
  0.0 84.7 jit_solution(10018292500827125171)
XLA Ops:
  0.0 0.9 %constant_dynamic-update-slice_fusion.1 = (bf16[256,256]{1,0:T(8,128)(2,1)S(1)}, bf16[2048,256]{1,0:T(8,128)(2,1)S(1)}) fusion(bf16[256,128]{1,0:T(8,128)(2,1)} %param.6), kind=kLoop, calls=%fused_computation.18 | loop fusion | bytes 196608
  0.9 0.9 %constant_dynamic-update-slice_fusion = (bf16[256,256]{1,0:T(8,128)(2,1)S(1)}, bf16[2048,256]{1,0:T(8,128)(2,1)S(1)}) fusion(bf16[256,256]{1,0:T(8,128)(2,1)S(1)} %get-tuple-element.7, bf16[256,128]{1,0:T(8,128)(2,1)} %param.7, bf16[2048,256]{1,0:T(8,128)(2,1)S(1)} %get-tuple-element.8), kind=kLoop, calls=%fused_computation.17 | loop fusion | bytes 196608 | tf_op jit(solution)/shard_map/concatenate | solution.py:151
  1.7 3.7 %collective-permute-start = (bf16[256,256]{1,0:T(8,128)(2,1)S(1)}, bf16[256,256]{1,0:T(8,128)(2,1)S(1)}, u32[]{:S(2)}, u32[]{:S(2)}) collective-permute-start(bf16[256,256]{1,0:T(8,128)(2,1)S(1)} %get-tuple-element.5), channel_id=1, source_target_pairs={{0,64},{64,0},{1,65},{65,1},{2,66},{66,2},{3,67},{67,3},{4,68},{68... | collective-permute-start | bytes 393224 | tf_op jit(solution)/shard_map/ppermute | solution.py:37
  5.4 3.2 %collective-permute-done = bf16[256,256]{1,0:T(8,128)(2,1)S(1)} collective-permute-done((bf16[256,256]{1,0:T(8,128)(2,1)S(1)}, bf16[256,256]{1,0:T(8,128)(2,1)S(1)}, u32[]{:S(2)}, u32[]{:S(2)}) %collective-permute-start) | collective-permute-done | bytes 131104 | tf_op jit(solution)/shard_map/ppermute | solution.py:37
  8.7 0.1 collective-permute-start.1
  8.8 1.5 %collective-permute-start.2 = (bf16[512,256]{1,0:T(8,128)(2,1)S(1)}, bf16[512,256]{1,0:T(8,128)(2,1)S(1)}, u32[]{:S(2)}, u32[]{:S(2)}) collective-permute-start(bf16[512,256]{1,0:T(8,128)(2,1)S(1)} %pad_maximum_fusion), channel_id=1, source_target_pairs={{0,12},{1,49},{4,0},{5,53},{8,4},{9,57},{12,8},{13,61},{16,28},{17... | collective-permute-start | bytes 786440 | tf_op jit(solution)/shard_map/ppermute | solution.py:154
  10.2 1.0 %collective-permute-start.3 = (bf16[512,256]{1,0:T(8,128)(2,1)S(1)}, bf16[512,256]{1,0:T(8,128)(2,1)S(1)}, u32[]{:S(2)}, u32[]{:S(2)}) collective-permute-start(bf16[512,256]{1,0:T(8,128)(2,1)S(1)} %pad_maximum_fusion), channel_id=1, source_target_pairs={{0,8},{1,33},{4,12},{5,37},{8,0},{9,41},{12,4},{13,45},{16,24},{17... | collective-permute-start | bytes 786440 | tf_op jit(solution)/shard_map/ppermute | solution.py:154
  11.2 2.8 %collective-permute-done.1 = bf16[512,256]{1,0:T(8,128)(2,1)S(1)} collective-permute-done((bf16[512,256]{1,0:T(8,128)(2,1)S(1)}, bf16[512,256]{1,0:T(8,128)(2,1)S(1)}, u32[]{:S(2)}, u32[]{:S(2)}) %collective-permute-start.1) | collective-permute-done | bytes 262176 | tf_op jit(solution)/shard_map/ppermute | solution.py:154
  14.0 4.4 %collective-permute-done.2 = bf16[512,256]{1,0:T(8,128)(2,1)S(1)} collective-permute-done((bf16[512,256]{1,0:T(8,128)(2,1)S(1)}, bf16[512,256]{1,0:T(8,128)(2,1)S(1)}, u32[]{:S(2)}, u32[]{:S(2)}) %collective-permute-start.2) | collective-permute-done | bytes 262176 | tf_op jit(solution)/shard_map/ppermute | solution.py:154
  18.4 0.0 collective-permute-done.3
  18.4 1.1 %collective-permute-start.4 = (bf16[2048,256]{1,0:T(8,128)(2,1)S(1)}, bf16[2048,256]{1,0:T(8,128)(2,1)S(1)}, u32[]{:S(2)}, u32[]{:S(2)}) collective-permute-start(bf16[2048,256]{1,0:T(8,128)(2,1)S(1)} %constant_dynamic-update-slice_fusion.2.b0), channel_id=1, source_target_pairs={{0,16},{1,5},{4,20},{5,9},{8,24},{9,13},{12,28},{13,1},{16,32},{17... | collective-permute-start | bytes 3145736 | tf_op jit(solution)/shard_map/ppermute | solution.py:156
  19.5 1.6 %collective-permute-start.5 = (bf16[2048,256]{1,0:T(8,128)(2,1)S(1)}, bf16[2048,256]{1,0:T(8,128)(2,1)}, u32[]{:S(2)}, u32[]{:S(2)}) collective-permute-start(bf16[2048,256]{1,0:T(8,128)(2,1)S(1)} %constant_dynamic-update-slice_fusion.2.b0), channel_id=1, source_target_pairs={{0,48},{1,13},{4,52},{5,1},{8,56},{9,5},{12,60},{13,9},{16,0},{17,... | collective-permute-start | bytes 3145736 | tf_op jit(solution)/shard_map/ppermute | solution.py:156
  21.2 1.4 %collective-permute-start.6 = (bf16[2048,256]{1,0:T(8,128)(2,1)S(1)}, bf16[2048,256]{1,0:T(8,128)(2,1)}, u32[]{:S(2)}, u32[]{:S(2)}) collective-permute-start(bf16[2048,256]{1,0:T(8,128)(2,1)S(1)} %constant_dynamic-update-slice_fusion.2.b0), channel_id=1, source_target_pairs={{0,32},{1,9},{4,36},{5,13},{8,40},{9,1},{12,44},{13,5},{16,48},{17... | collective-permute-start | bytes 3145736 | tf_op jit(solution)/shard_map/ppermute | solution.py:156
  22.5 0.1 pad_add_fusion.place
  22.6 11.1 %collective-permute-done.4.b1 = bf16[2048,256]{1,0:T(8,128)(2,1)S(1)} collective-permute-done((bf16[2048,256]{1,0:T(8,128)(2,1)S(1)}, bf16[2048,256]{1,0:T(8,128)(2,1)S(1)}, u32[]{:S(2)}, u32[]{:S(2)}) %collective-permute-start.4) | collective-permute-done | bytes 1048608 | tf_op jit(solution)/shard_map/ppermute | solution.py:156
  33.7 10.4 %collective-permute-done.5.b2 = bf16[2048,256]{1,0:T(8,128)(2,1)} collective-permute-done((bf16[2048,256]{1,0:T(8,128)(2,1)S(1)}, bf16[2048,256]{1,0:T(8,128)(2,1)}, u32[]{:S(2)}, u32[]{:S(2)}) %collective-permute-start.5) | collective-permute-done | bytes 1048608 | tf_op jit(solution)/shard_map/ppermute | solution.py:156
  44.1 1.8 %collective-permute-done.6.b3 = bf16[2048,256]{1,0:T(8,128)(2,1)} collective-permute-done((bf16[2048,256]{1,0:T(8,128)(2,1)S(1)}, bf16[2048,256]{1,0:T(8,128)(2,1)}, u32[]{:S(2)}, u32[]{:S(2)}) %collective-permute-start.6) | collective-permute-done | bytes 1048608 | tf_op jit(solution)/shard_map/ppermute | solution.py:156
  46.0 0.0 copy-start
  46.0 1.0 %copy-done = bf16[256,896]{1,0:T(8,128)(2,1)S(1)} copy-done((bf16[256,896]{1,0:T(8,128)(2,1)S(1)}, bf16[256,896]{1,0:T(8,128)(2,1)}, u32[]{:S(2)}) %copy-start) | copy-done | bytes 458776
  47.0 0.0 copy-start.1
  47.0 0.7 copy-done.1
  47.6 14.8 %shard_map.55 = bf16[256,896]{1,0:T(8,128)(2,1)S(1)} custom-call(s32[16]{0:T(128)S(1)} %copy-done.1, s32[4]{0:T(128)S(1)} %pad_add_fusion.place, bf16[256,896]{1,0:T(8,128)(2,1)S(1)} %copy-done, bf16[2048,256]{1,0:T(8,128)(2,1)S(1)} %constant_dynamic-update-slice_fusion.2.b0, bf16[2048,256]{1,0:T(8,128)(2,1)S(1)} %collective-permute-done.4.b1, ...), custom_call_target="tpu_custom_call" | custom-call | tf_op jit(solution)/shard_map/pallas_call | solution.py:133
  62.4 0.8 collective-permute-start.8
  63.2 3.6 %collective-permute-start.7 = (bf16[256,896]{1,0:T(8,128)(2,1)S(1)}, bf16[256,896]{1,0:T(8,128)(2,1)S(1)}, u32[]{:S(2)}, u32[]{:S(2)}) collective-permute-start(bf16[256,896]{1,0:T(8,128)(2,1)S(1)} %shard_map.55), channel_id=1, source_target_pairs={{0,1},{1,0},{2,3},{3,2},{4,5},{5,4},{6,7},{7,6},{8,9},{9,8},{10,11... | collective-permute-start | bytes 1376264 | tf_op jit(solution)/shard_map/ppermute | solution.py:37
  66.8 4.6 %collective-permute-done.8 = bf16[256,896]{1,0:T(8,128)(2,1)S(1)} collective-permute-done((bf16[256,896]{1,0:T(8,128)(2,1)S(1)}, bf16[256,896]{1,0:T(8,128)(2,1)S(1)}, u32[]{:S(2)}, u32[]{:S(2)}) %collective-permute-start.8) | collective-permute-done | bytes 458784 | tf_op jit(solution)/shard_map/ppermute | solution.py:37
  71.5 4.0 %collective-permute-start.9 = (bf16[256,896]{1,0:T(8,128)(2,1)S(1)}, bf16[256,896]{1,0:T(8,128)(2,1)S(1)}, u32[]{:S(2)}, u32[]{:S(2)}) collective-permute-start(bf16[256,896]{1,0:T(8,128)(2,1)S(1)} %collective-permute-done.8), channel_id=1, source_target_pairs={{0,1},{1,0},{2,3},{3,2},{4,5},{5,4},{6,7},{7,6},{8,9},{9,8},{10,11... | collective-permute-start | bytes 1376264 | tf_op jit(solution)/shard_map/ppermute | solution.py:37
  75.4 2.1 %fusion.2 = f32[256,896]{1,0:T(8,128)S(1)} fusion(bf16[256,896]{1,0:T(8,128)(2,1)S(1)} %collective-permute-done.8, bf16[4,896,896]{2,1,0:T(8,128)(2,1)} %bitcast.29, s32[]{:T(128)S(6)} %select_n.15), kind=kOutput, calls=%fused_computation.2 | convolution fusion | flops 411041792 | bytes 2981892 | tf_op jit(solution)/shard_map/dot_general | solution.py:165
  77.5 0.0 collective-permute-done.7
  77.6 2.1 %fusion.4 = f32[256,896]{1,0:T(8,128)S(1)} fusion(bf16[256,896]{1,0:T(8,128)(2,1)S(1)} %collective-permute-done.7, bf16[4,896,896]{2,1,0:T(8,128)(2,1)} %bitcast.30, s32[]{:T(128)S(6)} %select_n.14), kind=kOutput, calls=%fused_computation.4 | convolution fusion | flops 411041792 | bytes 2981892 | tf_op jit(solution)/shard_map/dot_general | solution.py:165
  79.7 2.1 %fusion.15 = f32[256,896]{1,0:T(8,128)S(1)} fusion(f32[256,896]{1,0:T(8,128)S(1)} %fusion.2, f32[256,896]{1,0:T(8,128)S(1)} %fusion.4, bf16[256,896]{1,0:T(8,128)(2,1)S(1)} %shard_map.55, bf16[4,896,896]{2,1,0:T(8,128)(2,1)} %bitcast.31, s32[]{:T(128)S(6)} %select_n.13), kind=kOutput, calls=%fused_computation.13 | convolution fusion | flops 411500544 | bytes 4816900 | tf_op jit(solution)/shard_map/dot_general | solution.py:165
  81.8 0.0 collective-permute-done.9
  81.8 2.9 %fusion.21 = bf16[256,896]{1,0:T(8,128)(2,1)} fusion(f32[256,896]{1,0:T(8,128)S(1)} %fusion.15, bf16[256,896]{1,0:T(8,128)(2,1)S(1)} %collective-permute-done.9, bf16[4,896,896]{2,1,0:T(8,128)(2,1)} %bitcast.32, s32[]{:T(128)S(6)} %select_n.16), kind=kOutput, calls=%fused_computation.15 | convolution fusion | flops 411500544 | bytes 3440644 | tf_op jit(solution)/shard_map/dot_general | solution.py:165
  (5 shorter events, 0.1 us)
Async XLA Ops:
  1.7 6.9 %collective-permute-start = (bf16[256,256]{1,0:T(8,128)(2,1)S(1)}, bf16[256,256]{1,0:T(8,128)(2,1)S(1)}, u32[]{:S(2)}, u32[]{:S(2)}) collective-permute-start(bf16[256,256]{1,0:T(8,128)(2,1)S(1)} %get-tuple-element.5), channel_id=1, source_target_pairs={{0,64},{64,0},{1,65},{65,1},{2,66},{66,2},{3,67},{67,3},{4,68},{68... | collective-permute-start | bytes 393224 | tf_op jit(solution)/shard_map/ppermute | solution.py:37
  8.7 5.3 %collective-permute-start.1 = (bf16[512,256]{1,0:T(8,128)(2,1)S(1)}, bf16[512,256]{1,0:T(8,128)(2,1)S(1)}, u32[]{:S(2)}, u32[]{:S(2)}) collective-permute-start(bf16[512,256]{1,0:T(8,128)(2,1)S(1)} %pad_maximum_fusion), channel_id=1, source_target_pairs={{0,4},{1,17},{4,8},{5,21},{8,12},{9,25},{12,0},{13,29},{16,20},{17... | collective-permute-start | bytes 786440 | tf_op jit(solution)/shard_map/ppermute | solution.py:154
  8.8 9.6 %collective-permute-start.2 = (bf16[512,256]{1,0:T(8,128)(2,1)S(1)}, bf16[512,256]{1,0:T(8,128)(2,1)S(1)}, u32[]{:S(2)}, u32[]{:S(2)}) collective-permute-start(bf16[512,256]{1,0:T(8,128)(2,1)S(1)} %pad_maximum_fusion), channel_id=1, source_target_pairs={{0,12},{1,49},{4,0},{5,53},{8,4},{9,57},{12,8},{13,61},{16,28},{17... | collective-permute-start | bytes 786440 | tf_op jit(solution)/shard_map/ppermute | solution.py:154
  10.2 8.2 %collective-permute-start.3 = (bf16[512,256]{1,0:T(8,128)(2,1)S(1)}, bf16[512,256]{1,0:T(8,128)(2,1)S(1)}, u32[]{:S(2)}, u32[]{:S(2)}) collective-permute-start(bf16[512,256]{1,0:T(8,128)(2,1)S(1)} %pad_maximum_fusion), channel_id=1, source_target_pairs={{0,8},{1,33},{4,12},{5,37},{8,0},{9,41},{12,4},{13,45},{16,24},{17... | collective-permute-start | bytes 786440 | tf_op jit(solution)/shard_map/ppermute | solution.py:154
  18.4 15.3 %collective-permute-start.4 = (bf16[2048,256]{1,0:T(8,128)(2,1)S(1)}, bf16[2048,256]{1,0:T(8,128)(2,1)S(1)}, u32[]{:S(2)}, u32[]{:S(2)}) collective-permute-start(bf16[2048,256]{1,0:T(8,128)(2,1)S(1)} %constant_dynamic-update-slice_fusion.2.b0), channel_id=1, source_target_pairs={{0,16},{1,5},{4,20},{5,9},{8,24},{9,13},{12,28},{13,1},{16,32},{17... | collective-permute-start | bytes 3145736 | tf_op jit(solution)/shard_map/ppermute | solution.py:156
  19.5 24.6 %collective-permute-start.5 = (bf16[2048,256]{1,0:T(8,128)(2,1)S(1)}, bf16[2048,256]{1,0:T(8,128)(2,1)}, u32[]{:S(2)}, u32[]{:S(2)}) collective-permute-start(bf16[2048,256]{1,0:T(8,128)(2,1)S(1)} %constant_dynamic-update-slice_fusion.2.b0), channel_id=1, source_target_pairs={{0,48},{1,13},{4,52},{5,1},{8,56},{9,5},{12,60},{13,9},{16,0},{17,... | collective-permute-start | bytes 3145736 | tf_op jit(solution)/shard_map/ppermute | solution.py:156
  21.2 24.8 %collective-permute-start.6 = (bf16[2048,256]{1,0:T(8,128)(2,1)S(1)}, bf16[2048,256]{1,0:T(8,128)(2,1)}, u32[]{:S(2)}, u32[]{:S(2)}) collective-permute-start(bf16[2048,256]{1,0:T(8,128)(2,1)S(1)} %constant_dynamic-update-slice_fusion.2.b0), channel_id=1, source_target_pairs={{0,32},{1,9},{4,36},{5,13},{8,40},{9,1},{12,44},{13,5},{16,48},{17... | collective-permute-start | bytes 3145736 | tf_op jit(solution)/shard_map/ppermute | solution.py:156
  46.0 1.0 %copy-start = (bf16[256,896]{1,0:T(8,128)(2,1)S(1)}, bf16[256,896]{1,0:T(8,128)(2,1)}, u32[]{:S(2)}) copy-start(bf16[256,896]{1,0:T(8,128)(2,1)} %queries.1) | copy-start | bytes 1376260
  47.0 0.7 copy-start.1
  62.4 9.0 %collective-permute-start.8 = (bf16[256,896]{1,0:T(8,128)(2,1)S(1)}, bf16[256,896]{1,0:T(8,128)(2,1)S(1)}, u32[]{:S(2)}, u32[]{:S(2)}) collective-permute-start(bf16[256,896]{1,0:T(8,128)(2,1)S(1)} %shard_map.55), channel_id=1, source_target_pairs={{0,2},{2,0},{1,3},{3,1},{4,6},{6,4},{5,7},{7,5},{8,10},{10,8},{9,1... | collective-permute-start | bytes 1376264 | tf_op jit(solution)/shard_map/ppermute | solution.py:37
  63.2 14.4 %collective-permute-start.7 = (bf16[256,896]{1,0:T(8,128)(2,1)S(1)}, bf16[256,896]{1,0:T(8,128)(2,1)S(1)}, u32[]{:S(2)}, u32[]{:S(2)}) collective-permute-start(bf16[256,896]{1,0:T(8,128)(2,1)S(1)} %shard_map.55), channel_id=1, source_target_pairs={{0,1},{1,0},{2,3},{3,2},{4,5},{5,4},{6,7},{7,6},{8,9},{9,8},{10,11... | collective-permute-start | bytes 1376264 | tf_op jit(solution)/shard_map/ppermute | solution.py:37
  71.5 10.3 %collective-permute-start.9 = (bf16[256,896]{1,0:T(8,128)(2,1)S(1)}, bf16[256,896]{1,0:T(8,128)(2,1)S(1)}, u32[]{:S(2)}, u32[]{:S(2)}) collective-permute-start(bf16[256,896]{1,0:T(8,128)(2,1)S(1)} %collective-permute-done.8), channel_id=1, source_target_pairs={{0,1},{1,0},{2,3},{3,2},{4,5},{5,4},{6,7},{7,6},{8,9},{9,8},{10,11... | collective-permute-start | bytes 1376264 | tf_op jit(solution)/shard_map/ppermute | solution.py:37

commit v2 on v1

v2 whole, which is shorter than its diff:
```python
import functools

import jax
import jax.numpy as jnp
import numpy as np
from jax import lax
from jax.experimental import pallas as pl
from jax.experimental.pallas import tpu as pltpu
from jax.sharding import Mesh, PartitionSpec as P

HD = 128
GRAIN = 64
TOK = 256
HEADS = 7
GRAINS = TOK // GRAIN
DOCS = 16
LONG_GRAINS = 68
PLANE_GRAINS = 64
PLANE_TOK = PLANE_GRAINS * GRAIN
EXTRA = LONG_GRAINS - PLANE_GRAINS
PIECE = 4 * TOK
MESSAGE = PIECE + EXTRA * GRAIN
SMALL = 256
NEAR_BLOCKS = 3
FAR_BLOCKS = 9
CHUNKS = ((0, 4), (4, 7))
TILE = 896
FLAG = HEADS * TOK
SCALE = 1.4426950408889634 / HD**0.5
LOWEST = -1e30
SAFE = (90.0 / SCALE) ** 2
UNSAFE = 1e30
OFFSETS = (0, -1, 1, 2)

SMEM = pl.BlockSpec(memory_space=pltpu.SMEM)
VMEM = pl.BlockSpec(memory_space=pltpu.VMEM)
HBM = pl.BlockSpec(memory_space=pltpu.HBM)


def turn(by_first, by_second):
    pairs = []
    for y in range(4):
        for x in range(4):
            pairs.append((y, x, 0, (y + by_first) % 4, (x + by_second) % 4))
            pairs.append((y, x, 1, (y + by_second) % 4, (x + by_first) % 4))
    return [((y * 4 + x) * 2 + c, (to_y * 4 + to_x) * 2 + c) for y, x, c, to_y, to_x in pairs]


def move(block, by_first, by_second):
    return lax.ppermute(block, ("y", "x", "c"), turn(by_first, by_second))


def ring(block, step):
    pairs = []
    for at in range(16):
        pairs.append((at, (at + step) % 16))
        pairs.append((16 + at, 16 + (at - step) % 16))
    return lax.ppermute(block, ("zh", "y", "x"), pairs)


def swap(block, axis):
    return lax.ppermute(block, axis, [(0, 1), (1, 0)])


class Lengths:
    def __init__(self, table):
        self.table = table

    def __getitem__(self, doc):
        return self.table[4 + doc]


class Place:
    def __init__(self, table):
        lengths = Lengths(table)
        self.zh, y, x, self.core = table[0], table[1], table[2], table[3]
        self.inner = jnp.where(self.core == 0, x, y)
        self.outer = jnp.where(self.core == 0, y, x)
        self.position = y * 4 + x
        total, start = jnp.int32(0), jnp.int32(0)
        for doc in range(DOCS):
            start = jnp.where(lengths[doc] == LONG_GRAINS, total, start)
            total = total + lengths[doc]
        self.start, self.stop = start, start + EXTRA

    def at(self, outer_by, inner_by):
        outer, inner = (self.outer + outer_by + 4) % 4, (self.inner + inner_by + 4) % 4
        return jnp.where(self.core == 0, outer * 4 + inner, inner * 4 + outer)

    def has_long(self, position):
        return jnp.where(self.zh == 0, position * 4 + 3 >= self.start, position * 4 < self.stop)

    def has_small(self, position):
        return jnp.where(self.zh == 0, position * 4 < self.start, position * 4 + 3 >= self.stop)


def rows_of(start, count):
    return pl.ds(pl.multiple_of(start, GRAIN), count)


def bounds(lengths, grain):
    first, end, total = jnp.int32(0), jnp.int32(0), jnp.int32(0)
    for doc in range(DOCS):
        after = total + lengths[doc]
        inside = (total <= grain) & (grain < after)
        first = jnp.where(inside, total, first)
        end = jnp.where(inside, after, end)
        total = after
    return first, end


def join_kernel(keys, values, out, sems):
    copies = [
        pltpu.make_async_copy(keys, out.at[:, pl.ds(0, HD)], sems.at[0]),
        pltpu.make_async_copy(values, out.at[:, pl.ds(HD, HD)], sems.at[1]),
    ]
    for copy in copies:
        copy.start()
    for copy in copies:
        copy.wait()


def join(keys, values):
    return pl.pallas_call(
        join_kernel,
        out_shape=jax.ShapeDtypeStruct((TOK, 2 * HD), jnp.bfloat16),
        in_specs=[HBM, HBM],
        out_specs=VMEM,
        scratch_shapes=[pltpu.SemaphoreType.DMA((2,))],
        name="join",
    )(keys, values)


def pack_kernel(table, *refs):
    natives, others, (own, m1, m2, m3, far) = refs[:4], refs[4:8], refs[-5:]
    here = Place(table)
    for inner in range(4):
        cut = jnp.clip(here.start - here.at(0, OFFSETS[inner]) * 4, 0, 4)
        for plane, blocks in ((here.zh, natives), (1 - here.zh, others)):
            @pl.when(cut == 4 * plane)
            def _():
                own[pl.ds(inner * TOK, TOK), :] = blocks[inner][...]

            @pl.when((cut > 0) & (cut < 4))
            def _():
                for grain in range(GRAINS):
                    @pl.when((grain < cut).astype(jnp.int32) == plane)
                    def _():
                        own[pl.ds(inner * TOK + grain * GRAIN, GRAIN), :] = blocks[inner][
                            pl.ds(grain * GRAIN, GRAIN), :]

    for extra in range(EXTRA):
        grain = here.start + extra
        for inner in range(4):
            for plane, blocks in ((1, natives), (0, others)):
                @pl.when((grain // 4 == here.at(0, OFFSETS[inner])) & (here.zh == plane))
                def _():
                    own[pl.ds(PIECE + extra * GRAIN, GRAIN), :] = blocks[inner][
                        rows_of(grain % 4 * GRAIN, GRAIN), :]

    for index, out in enumerate((m1, m2, m3)):
        to_long = here.has_long(here.at(-OFFSETS[index + 1], 0))

        @pl.when(to_long)
        def _():
            out[...] = own[...]

        @pl.when(jnp.logical_not(to_long))
        def _():
            for inner in range(4):
                out[pl.ds(inner * TOK, TOK), :] = natives[inner][...]

    lengths = Lengths(table)
    start, end = here.start, here.start + LONG_GRAINS
    before, after = start - start % 4, end + (4 - end % 4) % 4
    reach_before = jnp.where(start % 4 == 0, 0, before - bounds(lengths, before)[0])
    reach_after = jnp.where(end % 4 == 0, 0, bounds(lengths, after - 1)[1] - after)
    far[0] = (jnp.maximum(reach_before, reach_after) > NEAR_BLOCKS * 4).astype(jnp.int32)


def pack(table, natives, others, after):
    return pl.pallas_call(
        pack_kernel,
        out_shape=[jax.ShapeDtypeStruct((MESSAGE, 2 * HD), jnp.bfloat16)] * 4 + [
            jax.ShapeDtypeStruct((1,), jnp.int32)],
        in_specs=[SMEM] + [VMEM] * 8 + [HBM] * len(after),
        out_specs=[VMEM] * 4 + [SMEM],
        compiler_params=PARAMS,
        name="pack",
    )(table, *natives, *others, *after)


def put(block, keys, values, rows):
    keys[rows, :] = block[:, :HD]
    values[rows, :HD] = block[:, HD:]


def ones_beside(values):
    values[:, HD:] = jnp.ones((values.shape[0], HD), jnp.bfloat16)


def largest_square(block):
    block = block.astype(jnp.float32)
    return jnp.max(jnp.sum(block * block, axis=1, keepdims=True))


def plain_step(summed, query, keys, values):
    scores = lax.dot_general(
        query, keys, (((1,), (1,)), ((), ())), preferred_element_type=jnp.float32
    )
    weights = jnp.exp2(scores * SCALE).astype(jnp.bfloat16)
    product = jnp.dot(weights, values, preferred_element_type=jnp.float32)
    return product if summed is None else summed + product


def softmax_step(peak, summed, query, keys, values, allowed=None):
    scores = lax.dot_general(
        query, keys, (((1,), (1,)), ((), ())), preferred_element_type=jnp.float32
    )
    scores = scores * SCALE
    if allowed is not None:
        scores = jnp.where(allowed, scores, LOWEST)
    top = jnp.max(scores, axis=1, keepdims=True)
    peak_new = top if peak is None else jnp.maximum(peak, top)
    weights = jnp.exp2(scores - peak_new).astype(jnp.bfloat16)
    product = jnp.dot(weights, values, preferred_element_type=jnp.float32)
    if peak is not None:
        product = summed * jnp.exp2(peak - peak_new) + product
    return peak_new, product


def stacked(queries, heads, start, count):
    return jnp.concatenate(
        [queries[pl.ds(start, count), pl.ds(head * HD, HD)] for head in heads], axis=0
    )


def own_kernel(table, queries, own, rows_out, peak_out, summed_out, keys, values):
    here = Place(table)

    @pl.when(here.has_long(here.position))
    def _():
        for head in range(HEADS):
            rows_out[pl.ds(head * TOK, TOK), :] = queries[:, pl.ds(head * HD, HD)]
        ones_beside(values)
        put(own[pl.ds(0, PIECE), :], keys, values, pl.ds(0, PIECE))
        queries_square = largest_square(rows_out[...])
        plain = queries_square * largest_square(keys[...]) <= SAFE
        peak_out[pl.ds(FLAG, 8), :] = jnp.full((8, HD), jnp.where(plain, queries_square, UNSAFE))

        @pl.when(plain)
        def _():
            peak_out[pl.ds(0, FLAG), :] = jnp.zeros((FLAG, HD), jnp.float32)

            def tile(index, carry):
                rows = pl.ds(pl.multiple_of(index * TILE, TILE), TILE)
                summed_out[rows, :] = plain_step(None, rows_out[rows, :], keys[...], values[...])
                return carry

            lax.fori_loop(0, FLAG // TILE, tile, 0)

        @pl.when(jnp.logical_not(plain))
        def _():
            def tile(index, carry):
                rows = pl.ds(pl.multiple_of(index * TOK, TOK), TOK)
                peak, summed = softmax_step(None, None, rows_out[rows, :], keys[...], values[...])
                peak_out[rows, :] = jnp.broadcast_to(peak, (TOK, HD))
                summed_out[rows, :] = summed
                return carry

            lax.fori_loop(0, HEADS, tile, 0)


def still_plain(peak, keys):
    return jnp.max(peak[pl.ds(FLAG, 8), :]) * largest_square(keys[...]) <= SAFE


def middle_kernel(
    table, queries, b1, b2, peak_in, summed_in, peak_out, summed_out, keys, values
):
    here = Place(table)

    @pl.when(here.has_long(here.position))
    def _():
        ones_beside(values)
        for index, message in enumerate((b1, b2)):
            put(message[pl.ds(0, PIECE), :], keys, values, pl.ds(index * PIECE, PIECE))
        plain = still_plain(peak_in, keys)

        @pl.when(plain)
        def _():
            def tile(index, carry):
                rows = pl.ds(pl.multiple_of(index * TILE, TILE), TILE)
                query, summed = queries[rows, :], summed_in[rows, :]
                for part in (pl.ds(0, PIECE), pl.ds(PIECE, PIECE)):
                    summed = plain_step(summed, query, keys[part, :], values[part, :])
                summed_out[rows, :] = summed
                return carry

            lax.fori_loop(0, FLAG // TILE, tile, 0)

        @pl.when(jnp.logical_not(plain))
        def _():
            def tile(index, carry):
                rows = pl.ds(pl.multiple_of(index * TOK, TOK), TOK)
                peak, summed = softmax_step(
                    peak_in[rows, :1], summed_in[rows, :], queries[rows, :], keys[...], values[...])
                peak_out[rows, :] = jnp.broadcast_to(peak, (TOK, HD))
                summed_out[rows, :] = summed
                return carry

            lax.fori_loop(0, HEADS, tile, 0)
            peak_out[pl.ds(FLAG, 8), :] = jnp.full((8, HD), UNSAFE, jnp.float32)


def last_kernel(low, high, table, rows_in, own, b1, b2, b3, small, peak_in, summed_in, *refs):
    here = Place(table)
    count = high - low
    if low == 0:
        queries, n0, n1, n2, n3, out, rest, keys, values, result, held, *small_scratch = refs
        pure = jnp.logical_not(here.has_long(here.position))

        @pl.when(jnp.logical_not(pure))
        def _():
            held[...] = small[...]

        small_kernel(
            False, table, queries, n0, n1, n2, n3, b1, b2, b3, held, *small_scratch)
        small = held
        rest[...] = held[:, pl.ds(high * HD, (HEADS - high) * HD)]
    else:
        out, keys, values, result = refs[-4:]

    @pl.when(here.has_long(here.position))
    def _():
        ones_beside(values)
        put(b3[pl.ds(0, PIECE), :], keys, values, pl.ds(0, PIECE))
        for extra in range(EXTRA):
            grain = here.start + extra
            rows = pl.ds(PIECE + extra * GRAIN, GRAIN)
            group = jnp.where(here.core == 0, grain // 16, grain // 4 % 4)
            for message, by in zip((own, b1, b2, b3), OFFSETS):
                @pl.when(group == (here.outer + by + 4) % 4)
                def _():
                    put(message[rows, :], keys, values, rows)

        plain = still_plain(peak_in, keys)

        @pl.when(plain)
        def _():
            rows = pl.ds(low * TOK, count * TOK)
            summed = plain_step(summed_in[rows, :], rows_in[rows, :], keys[...], values[...])
            result[...] = (summed[:, :HD] / summed[:, HD:]).astype(jnp.bfloat16)

        @pl.when(jnp.logical_not(plain))
        def _():
            def tile(index, carry):
                rows = pl.ds(pl.multiple_of((low + index) * TOK, TOK), TOK)
                _, summed = softmax_step(
                    peak_in[rows, :1], summed_in[rows, :], rows_in[rows, :], keys[...], values[...])
                result[pl.ds(pl.multiple_of(index * TOK, TOK), TOK), :] = (
                    summed[:, :HD] / summed[:, HD:]).astype(jnp.bfloat16)
                return carry

            lax.fori_loop(0, count, tile, 0)

        for index in range(count):
            out[:, pl.ds(index * HD, HD)] = result[pl.ds(index * TOK, TOK), :]

    for grain in range(GRAINS):
        at = here.position * GRAINS + grain
        tokens = pl.ds(grain * GRAIN, GRAIN)

        @pl.when(jnp.where(here.zh == 0, at < here.start, at >= here.stop))
        def _():
            columns = pl.ds(0, count * HD)
            out[tokens, :] = small[tokens, columns]


def small_kernel(straddle, table, *refs):
    if straddle:
        far, queries, n0, r1, r2, r3, r4, _, out = refs[:9]
    else:
        queries, n0, n1, n2, n3, b1, b2, b3, out = refs[:9]
    keys, values, result = refs[-3:]
    here, lengths = Place(table), Lengths(table)
    long_here, small_here = here.has_long(here.position), here.has_small(here.position)

    @pl.when(small_here & (long_here if straddle else jnp.logical_not(long_here)))
    def _():
        def block(source, row, position):
            put(source[pl.ds(row, TOK), :], keys, values, rows_of(position * TOK, TOK))

        ones_beside(values)
        if straddle:
            values[:, :HD] = jnp.zeros((PLANE_TOK + SMALL, HD), jnp.bfloat16)
            block(n0, 0, here.position)
            away = jnp.where(here.zh == 0, -1, 1)
            for step in range(1, 1 + NEAR_BLOCKS + FAR_BLOCKS):
                position = here.position + away * step
                inside = (position >= 0) & (position < 16)
                source, row = ((r1, r2, r3)[step - 1], 0) if step <= NEAR_BLOCKS else (
                    r4, (step - 1 - NEAR_BLOCKS) * TOK)
                if step > NEAR_BLOCKS:
                    inside = inside & (far[0] == 1)

                @pl.when(inside)
                def _():
                    block(source, row, position)
        else:
            values[pl.ds(PLANE_TOK, SMALL), :HD] = jnp.zeros((SMALL, HD), jnp.bfloat16)
            for inner, near in enumerate(OFFSETS):
                block((n0, n1, n2, n3)[inner], 0, here.at(0, near))
                for message, by in zip((b1, b2, b3), OFFSETS[1:]):
                    block(message, inner * TOK, here.at(by, near))

        column = lax.broadcasted_iota(jnp.int32, (1, SMALL), 1)

        def one_grain(grain, carry):
            first, end = bounds(lengths, (here.zh * 16 + here.position) * GRAINS + grain)

            @pl.when(end - first != LONG_GRAINS)
            def _():
                tokens = rows_of(grain * GRAIN, GRAIN)
                query = stacked(queries, range(HEADS), tokens.start, GRAIN)
                offset = (first - here.zh * PLANE_GRAINS) * GRAIN
                width = (end - first) * GRAIN

                def step(index, state):
                    part = rows_of(offset + index * SMALL, SMALL)
                    return softmax_step(
                        *state, query, keys[part, :], values[part, :],
                        column < width - index * SMALL)

                initial = (
                    jnp.full((HEADS * GRAIN, 1), LOWEST, jnp.float32),
                    jnp.zeros((HEADS * GRAIN, 2 * HD), jnp.float32),
                )
                _, summed = lax.fori_loop(0, (width + SMALL - 1) // SMALL, step, initial)
                result[...] = (summed[:, :HD] / summed[:, HD:]).astype(jnp.bfloat16)
                for head in range(HEADS):
                    out[tokens, pl.ds(head * HD, HD)] = result[pl.ds(head * GRAIN, GRAIN), :]

            return carry

        lax.fori_loop(0, GRAINS, one_grain, 0)


def scratch(rows):
    return [pltpu.VMEM((rows, HD), jnp.bfloat16), pltpu.VMEM((rows, 2 * HD), jnp.bfloat16)]


def cost(keys, heads=HEADS):
    rows = heads * TOK
    return pl.CostEstimate(
        flops=6 * rows * keys * HD, bytes_accessed=rows * HD * 4, transcendentals=rows * keys)


STATE = [
    jax.ShapeDtypeStruct((FLAG + 8, HD), jnp.float32),
    jax.ShapeDtypeStruct((HEADS * TOK, 2 * HD), jnp.float32),
]
PARAMS = pltpu.CompilerParams(vmem_limit_bytes=28 * 2**20)


def attend_own(table, queries, own):
    rows = jax.ShapeDtypeStruct((HEADS * TOK, HD), jnp.bfloat16)
    return pl.pallas_call(
        own_kernel,
        out_shape=[rows] + STATE,
        in_specs=[SMEM, VMEM, VMEM],
        out_specs=[VMEM] * 3,
        scratch_shapes=scratch(PIECE),
        compiler_params=PARAMS,
        cost_estimate=cost(PIECE),
        name="own",
    )(table, queries, own)


def attend_middle(table, rows, messages, state, weight, after):
    def kernel(*refs):
        middle_kernel(*refs[:6], *refs[8:])

    return pl.pallas_call(
        kernel,
        out_shape=STATE,
        in_specs=[SMEM] + [VMEM] * 6 + [HBM],
        out_specs=[VMEM] * 2,
        scratch_shapes=scratch(2 * PIECE),
        input_output_aliases={4: 0, 5: 1},
        compiler_params=PARAMS,
        cost_estimate=cost(2 * PIECE),
        name="middle",
    )(table, rows, *messages, *state, weight, after)


def attend_last(low, high, table, blocks, more):
    shapes = [jax.ShapeDtypeStruct((TOK, (high - low) * HD), jnp.bfloat16)]
    scratches = scratch(MESSAGE) + [pltpu.VMEM(((high - low) * TOK, HD), jnp.bfloat16)]
    if low == 0:
        shapes.append(jax.ShapeDtypeStruct((TOK, (HEADS - high) * HD), jnp.bfloat16))
        scratches += [pltpu.VMEM((TOK, HEADS * HD), jnp.bfloat16)] + scratch(PLANE_TOK + SMALL) + [
            pltpu.VMEM((HEADS * GRAIN, HD), jnp.bfloat16)]
    return pl.pallas_call(
        functools.partial(last_kernel, low, high),
        out_shape=shapes,
        in_specs=[SMEM] + [VMEM] * (len(blocks) + len(more)),
        out_specs=[VMEM] * len(shapes),
        scratch_shapes=scratches,
        compiler_params=PARAMS,
        cost_estimate=cost(MESSAGE, high - low),
        name="last",
    )(table, *blocks, *more)


def attend_small(scalars, blocks):
    return pl.pallas_call(
        functools.partial(small_kernel, True),
        out_shape=jax.ShapeDtypeStruct((TOK, HEADS * HD), jnp.bfloat16),
        in_specs=[SMEM] * len(scalars) + [VMEM] * len(blocks),
        out_specs=VMEM,
        scratch_shapes=scratch(PLANE_TOK + SMALL) + [pltpu.VMEM((HEADS * GRAIN, HD), jnp.bfloat16)],
        compiler_params=PARAMS,
        cost_estimate=cost(TOK),
        name="small",
    )(*scalars, *blocks)


def add_products(total, groups, weight, parts):
    for index, head, part in parts:
        rows = pl.ds(pl.multiple_of(groups[index] * HEADS * HD + head * HD, HD), part.shape[1])
        term = jnp.dot(part[...], weight[rows, :], preferred_element_type=jnp.float32)
        total = term if total is None else total + term
    return total


def project_kernel(where, groups, weight, *refs):
    parts, before, out = refs[:len(where)], refs[len(where):-1], refs[-1]
    total = before[0][...] if before else None
    total = add_products(total, groups, weight, [(*w, p) for w, p in zip(where, parts)])
    out[...] = total.astype(out.dtype)


def project(where, groups, weight, parts, before, dtype):
    depth = sum(part.shape[1] for part in parts)
    return pl.pallas_call(
        functools.partial(project_kernel, where),
        out_shape=jax.ShapeDtypeStruct((TOK, weight.shape[1]), dtype),
        in_specs=[SMEM] + [VMEM] * (1 + len(parts) + len(before)),
        out_specs=VMEM,
        compiler_params=pltpu.CompilerParams(vmem_limit_bytes=20 * 2**20),
        cost_estimate=pl.CostEstimate(
            flops=2 * TOK * depth * weight.shape[1], bytes_accessed=2 * depth * weight.shape[1],
            transcendentals=0),
        name="project",
    )(groups, weight, *parts, *before)


def per_device(queries, keys, values, doc_lengths, out_weight):
    zh, y, x, zl, c = (lax.axis_index(a) for a in ("zh", "y", "x", "zl", "c"))
    table = jnp.concatenate([jnp.stack([zh, y, x, c]).astype(jnp.int32), doc_lengths])
    native = join(keys, values)
    other = swap(native, "zh")
    natives = [native] + [move(native, 0, -k) for k in OFFSETS[1:]]
    others = [other] + [move(other, 0, -k) for k in OFFSETS[1:]]
    rings = [ring(native, step) for step in range(1, 1 + NEAR_BLOCKS)]
    own, *sent, is_far = pack(table, natives, others, rings)
    messages = [move(block, -k, 0) for block, k in zip(sent, OFFSETS[1:])]
    nothing = jnp.zeros((FAR_BLOCKS * TOK, 2 * HD), jnp.bfloat16)

    def fetch(block):
        def step(index, carry):
            block, blocks = carry
            block = ring(block, 1)
            at = jnp.maximum(index - NEAR_BLOCKS, 0) * TOK
            return block, lax.dynamic_update_slice_in_dim(blocks, block, at, 0)

        return lax.fori_loop(0, NEAR_BLOCKS + FAR_BLOCKS, step, (block, nothing))[1]

    beyond_rings = lax.cond(is_far[0] == 1, fetch, lambda block: nothing, native)
    rows, *state = attend_own(table, queries, own)
    small = attend_small((table, is_far), (queries, native, *rings, beyond_rings, rows))
    state = attend_middle(table, rows, messages[:2], state, out_weight, small)
    (first, middle), (second, _) = CHUNKS
    some, rest = attend_last(
        first, middle, table, (rows, own, *messages, small, *state), (queries, *natives))
    chunks = [some] + list(attend_last(
        second, HEADS, table, (rows, own, *messages, rest, *state), ()))
    across = [swap(part, "zl") for part in chunks]
    beside = [swap(part, "c") for part in chunks]
    group = (zl * 2 + c).astype(jnp.int32)
    groups = jnp.stack([group, group ^ 1, group ^ 2, group ^ 3])
    mixed = project(
        [(0, first), (0, second), (1, first), (1, second)], groups, out_weight, chunks + beside, [],
        jnp.float32)
    across, mixed = lax.optimization_barrier((across, mixed))
    beyond = [swap(part, "c") for part in across]
    mixed = project(
        [(2, first), (3, first)], groups, out_weight, [across[0], beyond[0]], [mixed], jnp.float32)
    return project(
        [(2, second), (3, second)], groups, out_weight, [across[1], beyond[1]], [mixed],
        jnp.bfloat16)


def solution(mesh):
    fine = Mesh(np.asarray(mesh.devices).reshape(2, 4, 4, 2, 2), ("zh", "y", "x", "zl", "c"))
    seq, kv = ("zh", "y", "x"), ("zl", "c")
    return jax.shard_map(
        per_device,
        mesh=fine,
        in_specs=(P(seq, kv), P(seq, kv), P(seq, kv), P(), P(None, kv)),
        out_specs=P(seq, kv),
        check_vma=False,
    )
```

time: 85.4 us -> 94.2 us (1.10)
  Pallas kernels: 14.8 us -> 42.2 us
  waiting for transfers between devices: 38.4 us -> 11.6 us
  starting transfers between devices: 18.7 us -> 31.3 us
  matrix products: 9.23 us -> 0 us
  local copies, waits for them, and re-layouts: 3.48 us -> 7.68 us
    pallas_call x1 -> x10, Pallas kernels: 14.8 us -> 42.2 us  [the longest x1 12.3 us: attend_middle(): pl.pallas_call(kernel, out_shape=STATE, in_specs=[SMEM] + [VMEM] * 6 + [H...]
    ppermute x6 -> x12, waiting for transfers between devices: 30.5 us -> 4.91 us  [the longest x9 4.59 us: move(): return lax.ppermute(block, ('y', 'x', 'c'), turn(by_first, by_second))]
    ppermute x6 -> x12, starting transfers between devices: 6.6 us -> 17.2 us  [the longest x9 14.3 us: move(): return lax.ppermute(block, ('y', 'x', 'c'), turn(by_first, by_second))]
    dot_general x4 -> x0, matrix products: 9.23 us -> none  [per_device(): jnp.dot(part, lax.dynamic_index_in_dim(weight, group ^ index, 0, keepdims...]
    unnamed x8 -> x38, local copies, waits for them, and re-layouts: 2.57 us -> 5.84 us
    ppermute x4 -> x7, starting transfers between devices: 12.1 us -> 14.1 us  [swap(): return lax.ppermute(block, axis, [(0, 1), (1, 0)])]
    ppermute x4 -> x7, waiting for transfers between devices: 7.86 us -> 6.7 us  [swap(): return lax.ppermute(block, axis, [(0, 1), (1, 0)])]
    broadcast_in_dim x0 -> x1, local copies, waits for them, and re-layouts: none -> 1.11 us  [per_device(): nothing = jnp.zeros((FAR_BLOCKS * TOK, 2 * HD), jnp.bfloat16)]
  transfers between devices with their start and end apart: 10 -> 19, of which waited for: 7 -> 5; matrix products, arithmetic and copies ran while one was open for 8% -> 2% of each run, Pallas kernels for 0% -> 31%
where the time goes in v2:
time: 94.2 us; the launch traced here: 93.8 us
  Pallas kernels  42.2 us (45%)
  starting transfers between devices  31.3 us (33%)
  waiting for transfers between devices  11.6 us (12%)
  local copies, waits for them, and re-layouts  7.68 us (8%)
    ppermute x9, starting transfers between devices, move(): return lax.ppermute(block, ('y', 'x', 'c'), turn(by_first, by_second))  14.3 us
    ppermute x7, starting transfers between devices, swap(): return lax.ppermute(block, axis, [(0, 1), (1, 0)])  14.1 us
    pallas_call x1, Pallas kernels, attend_middle(): pl.pallas_call(kernel, out_shape=STATE, in_specs=[SMEM] + [VMEM] * 6 + [H...  12.3 us
    pallas_call x2, Pallas kernels, attend_last(): pl.pallas_call(functools.partial(last_kernel, low, high), out_shape=shape...  11.6 us
    pallas_call x1, Pallas kernels, attend_own(): pl.pallas_call(own_kernel, out_shape=[rows] + STATE, in_specs=[SMEM, VMEM...  6.95 us
    ppermute x7, waiting for transfers between devices, swap(): return lax.ppermute(block, axis, [(0, 1), (1, 0)])  6.7 us
    unnamed x38, local copies, waits for them, and re-layouts  5.84 us
    pallas_call x3, Pallas kernels, project(): pl.pallas_call(functools.partial(project_kernel, where), out_shape=jax.Sh...  5.03 us
  transfers between devices with their start and end apart: 19, of which 5 were waited for; matrix products, arithmetic and copies ran while one was open for 2% of the time, Pallas kernels for 31%

profile of v2, /device:TPU:25, one launch (start us, length us, event | category | flops | bytes accessed | tf_op | source)
XLA Modules:
  0.0 93.8 jit_solution(8920252344392725648)
XLA Ops:
  0.0 1.5 %join.1.refs_0_.refs_2_.refs_1_ = bf16[256,256]{1,0:T(8,128)(2,1)} custom-call(bf16[256,128]{1,0:T(8,128)(2,1)} %keys.1, bf16[256,128]{1,0:T(8,128)(2,1)} %values.1), custom_call_target="tpu_custom_call" | custom-call | tf_op jit(solution)/shard_map/join/pallas_call | solution.py:124
  1.5 2.5 %collective-permute-start.10 = (bf16[256,256]{1,0:T(8,128)(2,1)}, bf16[256,256]{1,0:T(8,128)(2,1)S(1)}, u32[]{:S(2)}, u32[]{:S(2)}) collective-permute-start(bf16[256,256]{1,0:T(8,128)(2,1)} %join.1.refs_0_.refs_2_.refs_1_), channel_id=1, source_target_pairs={{0,12},{64,116},{4,16},{68,120},{8,20},{72,124},{12,24},{76,64},{1... | collective-permute-start | bytes 393224 | tf_op jit(solution)/shard_map/ppermute | solution.py:58
  4.1 0.3 collective-permute-start.9
  4.4 4.5 %collective-permute-start.4 = (bf16[256,256]{1,0:T(8,128)(2,1)}, bf16[256,256]{1,0:T(8,128)(2,1)S(1)}, u32[]{:S(2)}, u32[]{:S(2)}) collective-permute-start(bf16[256,256]{1,0:T(8,128)(2,1)} %join.1.refs_0_.refs_2_.refs_1_), channel_id=1, source_target_pairs={{0,64},{64,0},{1,65},{65,1},{2,66},{66,2},{3,67},{67,3},{4,68},{68... | collective-permute-start | bytes 393224 | tf_op jit(solution)/shard_map/ppermute | solution.py:62
  8.9 0.0 collective-permute-start.8
  8.9 3.2 %collective-permute-start.3 = (bf16[256,256]{1,0:T(8,128)(2,1)}, bf16[256,256]{1,0:T(8,128)(2,1)S(1)}, u32[]{:S(2)}, u32[]{:S(2)}) collective-permute-start(bf16[256,256]{1,0:T(8,128)(2,1)} %join.1.refs_0_.refs_2_.refs_1_), channel_id=1, source_target_pairs={{0,8},{1,33},{4,12},{5,37},{8,0},{9,41},{12,4},{13,45},{16,24},{17... | collective-permute-start | bytes 393224 | tf_op jit(solution)/shard_map/ppermute | solution.py:50
  12.2 0.0 collective-permute-done.10.refs_10_.refs_5_
  12.2 0.0 collective-permute-start.2
  12.2 0.0 collective-permute-done.9.refs_9_.refs_4_
  12.2 0.0 copy-start.13
  12.2 2.7 %collective-permute-start.1 = (bf16[256,256]{1,0:T(8,128)(2,1)}, bf16[256,256]{1,0:T(8,128)(2,1)S(1)}, u32[]{:S(2)}, u32[]{:S(2)}) collective-permute-start(bf16[256,256]{1,0:T(8,128)(2,1)} %join.1.refs_0_.refs_2_.refs_1_), channel_id=1, source_target_pairs={{0,4},{1,17},{4,8},{5,21},{8,12},{9,25},{12,0},{13,29},{16,20},{17... | collective-permute-start | bytes 393224 | tf_op jit(solution)/shard_map/ppermute | solution.py:50
  14.9 0.0 collective-permute-done.4.refs_4_
  14.9 0.0 collective-permute-start.7
  14.9 0.3 collective-permute-done.8.refs_8_.refs_3_
  15.2 1.0 %collective-permute-start.6 = (bf16[256,256]{1,0:T(8,128)(2,1)S(1)}, bf16[256,256]{1,0:T(8,128)(2,1)S(1)}, u32[]{:S(2)}, u32[]{:S(2)}) collective-permute-start(bf16[256,256]{1,0:T(8,128)(2,1)S(1)} %collective-permute-done.4.refs_4_), channel_id=1, source_target_pairs={{0,12},{1,49},{4,0},{5,53},{8,4},{9,57},{12,8},{13,61},{16,28},{17... | collective-permute-start | bytes 393224 | tf_op jit(solution)/shard_map/ppermute | solution.py:50
  16.2 0.0 collective-permute-done.3.refs_3_.refs_4_
  16.2 4.7 %collective-permute-start.5 = (bf16[256,256]{1,0:T(8,128)(2,1)S(1)}, bf16[256,256]{1,0:T(8,128)(2,1)S(1)}, u32[]{:S(2)}, u32[]{:S(2)}) collective-permute-start(bf16[256,256]{1,0:T(8,128)(2,1)S(1)} %collective-permute-done.4.refs_4_), channel_id=1, source_target_pairs={{0,4},{1,17},{4,8},{5,21},{8,12},{9,25},{12,0},{13,29},{16,20},{17... | collective-permute-start | bytes 393224 | tf_op jit(solution)/shard_map/ppermute | solution.py:50
  20.9 0.7 concatenate.3.table.refs_0_
  21.6 0.0 collective-permute-done.2.refs_2_.refs_3_
  21.6 0.0 collective-permute-done.1.refs_1_.refs_2_
  21.6 0.0 collective-permute-done.7.refs_7_
  21.7 1.7 %collective-permute-done.6.refs_6_ = bf16[256,256]{1,0:T(8,128)(2,1)S(1)} collective-permute-done((bf16[256,256]{1,0:T(8,128)(2,1)S(1)}, bf16[256,256]{1,0:T(8,128)(2,1)S(1)}, u32[]{:S(2)}, u32[]{:S(2)}) %collective-permute-start.6) | collective-permute-done | bytes 131104 | tf_op jit(solution)/shard_map/ppermute | solution.py:50
  23.4 0.0 collective-permute-done.5.refs_5_
  23.4 2.9 %pack.1 = (bf16[1280,256]{1,0:T(8,128)(2,1)S(1)}, bf16[1280,256]{1,0:T(8,128)(2,1)}, bf16[1280,256]{1,0:T(8,128)(2,1)}, bf16[1280,256]{1,0:T(8,128)(2,1)}, s32[1]{0:T(128)}) custom-call(s32[20]{0:T(128)S(1)} %concatenate.3.table.refs_0_, bf16[256,256]{1,0:T(8,128)(2,1)} %join.1.refs_0_.refs_2_.refs_1_, ...), custom_call_target="tpu_custom_call" | custom-call | tf_op jit(solution)/shard_map/pack/pallas_call | solution.py:182
  26.3 0.0 copy-done.11
  26.3 0.0 copy-done.13
  26.3 0.0 copy-done.5
  26.4 0.9 copy-done.1
  27.2 0.0 collective-permute-start.11
  27.2 2.7 %collective-permute-start.12 = (bf16[1280,256]{1,0:T(8,128)(2,1)}, bf16[1280,256]{1,0:T(8,128)(2,1)S(1)}, u32[]{:S(2)}, u32[]{:S(2)}) collective-permute-start(bf16[1280,256]{1,0:T(8,128)(2,1)} %get-tuple-element.91), channel_id=1, source_target_pairs={{0,48},{1,13},{4,52},{5,1},{8,56},{9,5},{12,60},{13,9},{16,0},{17,... | collective-permute-start | bytes 1966088 | tf_op jit(solution)/shard_map/ppermute | solution.py:50
  29.9 0.0 collective-permute-start.13
  30.5 1.1 %conditional.1 = (bf16[2304,256]{1,0:T(8,128)(2,1)}) conditional(s32[]{:T(128)} %bitcast.8, () %tuple.26, bf16[256,256]{1,0:T(8,128)(2,1)} %join.1.refs_0_.refs_2_.refs_1_), branch_computations={%region_0.0_spmd, %region_1.0_spmd} | conditional | flops 8 | bytes 2490649 | solution.py:580
  30.5 1.1 %broadcast_in_dim.4 = bf16[2304,256]{1,0:T(8,128)(2,1)} broadcast(bf16[]{:T(256)} %constant.50.clone), dimensions={} | broadcast | bytes 1179650 | tf_op jit(solution)/shard_map/broadcast_in_dim | solution.py:569
  31.6 1.1 %copy-done.2 = bf16[1280,256]{1,0:T(8,128)(2,1)S(1)} copy-done((bf16[1280,256]{1,0:T(8,128)(2,1)S(1)}, bf16[1280,256]{1,0:T(8,128)(2,1)}, u32[]{:S(2)}) %copy-start.2) | copy-done | bytes 655384
  32.7 1.0 %copy-done.4 = bf16[256,896]{1,0:T(8,128)(2,1)S(1)} copy-done((bf16[256,896]{1,0:T(8,128)(2,1)S(1)}, bf16[256,896]{1,0:T(8,128)(2,1)}, u32[]{:S(2)}) %copy-start.4) | copy-done | bytes 458776
  33.7 6.9 %own.1 = (bf16[1792,128]{1,0:T(8,128)(2,1)S(1)}, f32[1800,128]{1,0:T(8,128)S(1)}, f32[1792,256]{1,0:T(8,128)S(1)}) custom-call(s32[20]{0:T(128)S(1)} %concatenate.3.table.refs_0_, bf16[256,896]{1,0:T(8,128)(2,1)S(1)} %copy-done.4, bf16[1280,256]{1,0:T(8,128)(2,1)S(1)} %copy-done.2), custom_call_target="tpu_custom_call" | custom-call | flops 1409286144 | bytes 917504 | tf_op jit(solution)/shard_map/own/pallas_call | solution.py:468
  40.7 2.0 %small.1.refs_7_ = bf16[256,896]{1,0:T(8,128)(2,1)S(1)} custom-call(s32[20]{0:T(128)S(1)} %concatenate.3.table.refs_0_, s32[1]{0:T(128)} %get-tuple-element.93.refs_0_, bf16[256,896]{1,0:T(8,128)(2,1)S(1)} %copy-done.4, bf16[256,256]{1,0:T(8,128)(2,1)} %join.1.refs_0_.refs_2_.refs_1_, bf16[256,256]{1,0:T(8,128)(2,1)S(1)} %copy-done.16, ...), custom_call_target="tpu_custom_call" | custom-call | flops 352321536 | bytes 917504 | tf_op jit(solution)/shard_map/small/pallas_call | solution.py:517
  42.7 2.8 %collective-permute-done.11.refs_2_.b1 = bf16[1280,256]{1,0:T(8,128)(2,1)S(1)} collective-permute-done((bf16[1280,256]{1,0:T(8,128)(2,1)}, bf16[1280,256]{1,0:T(8,128)(2,1)S(1)}, u32[]{:S(2)}, u32[]{:S(2)}) %collective-permute-start.11) | collective-permute-done | bytes 655392 | tf_op jit(solution)/shard_map/ppermute | solution.py:50
  45.5 0.0 collective-permute-done.12.refs_3_.b2
  45.6 12.3 %middle.1 = (f32[1800,128]{1,0:T(8,128)S(1)}, f32[1792,256]{1,0:T(8,128)S(1)}) custom-call(s32[20]{0:T(128)S(1)} %concatenate.3.table.refs_0_, bf16[1792,128]{1,0:T(8,128)(2,1)S(1)} %get-tuple-element.89.refs_7_.refs_1_.rows_in, bf16[1280,256]{1,0:T(8,128)(2,1)S(1)} %collective-permute-done.11.refs_2_.b1, ...), custom_call_target="tpu_custom_call", output_to_operand_aliasing={{0}: (4, {}), {1}: (5, {})} | custom-call | flops 2818572288 | bytes 917504 | tf_op jit(solution)/shard_map/middle/pallas_call | solution.py:484
  57.8 0.0 collective-permute-done.13.b3
  57.8 0.0 copy-done.3
  57.8 0.0 copy-done.6
  57.9 0.0 copy-done.8
  57.9 0.0 copy-done.10
  57.9 6.5 %last.2 = (bf16[256,512]{1,0:T(8,128)(2,1)S(1)}, bf16[256,384]{1,0:T(8,128)(2,1)S(1)}) custom-call(s32[20]{0:T(128)S(1)} %concatenate.3.table.refs_0_, bf16[1792,128]{1,0:T(8,128)(2,1)S(1)} %get-tuple-element.89.refs_7_.refs_1_.rows_in, bf16[1280,256]{1,0:T(8,128)(2,1)S(1)} %copy-done.3, bf16[1280,256]{1,0:T(8,128)(2,1)S(1)} %collective-permute-done.11.refs_2_.b1, ...), custom_call_target="tpu_custom_call" | custom-call | flops 1006632960 | bytes 524288 | tf_op jit(solution)/shard_map/last/pallas_call | solution.py:504
  64.3 6.7 %collective-permute-start.16 = (bf16[256,512]{1,0:T(8,128)(2,1)S(1)}, bf16[256,512]{1,0:T(8,128)(2,1)S(1)}, u32[]{:S(2)}, u32[]{:S(2)}) collective-permute-start(bf16[256,512]{1,0:T(8,128)(2,1)S(1)} %get-tuple-element.98.refs_0_), channel_id=1, source_target_pairs={{0,1},{1,0},{2,3},{3,2},{4,5},{5,4},{6,7},{7,6},{8,9},{9,8},{10,11... | collective-permute-start | bytes 786440 | tf_op jit(solution)/shard_map/ppermute | solution.py:62
  71.1 5.2 %last.3.refs_1_ = bf16[256,384]{1,0:T(8,128)(2,1)S(1)} custom-call(s32[20]{0:T(128)S(1)} %concatenate.3.table.refs_0_, bf16[1792,128]{1,0:T(8,128)(2,1)S(1)} %get-tuple-element.89.refs_7_.refs_1_.rows_in, bf16[1280,256]{1,0:T(8,128)(2,1)S(1)} %copy-done.3, bf16[1280,256]{1,0:T(8,128)(2,1)S(1)} %collective-permute-done.11.refs_2_.b1, ...), custom_call_target="tpu_custom_call" | custom-call | flops 754974720 | bytes 393216 | tf_op jit(solution)/shard_map/last/pallas_call | solution.py:504
  76.3 0.1 collective-permute-start.17
  76.4 0.8 collective-permute-start.14
  77.1 0.8 collective-permute-start.15
  77.9 0.1 pad_add_fusion.groups
  78.0 0.0 collective-permute-done.17.refs_3_
  78.0 0.0 collective-permute-done.16.refs_2_
  78.0 2.8 %copy-done = bf16[3584,896]{1,0:T(8,128)(2,1)S(1)} copy-done((bf16[3584,896]{1,0:T(8,128)(2,1)S(1)}, bf16[3584,896]{1,0:T(8,128)(2,1)}, u32[]{:S(2)}) %copy-start) | copy-done | bytes 6422552
  80.8 1.8 %project.3.refs_2_ = f32[256,896]{1,0:T(8,128)S(1)} custom-call(s32[4]{0:T(128)S(1)} %pad_add_fusion.groups, bf16[3584,896]{1,0:T(8,128)(2,1)S(1)} %copy-done, bf16[256,512]{1,0:T(8,128)(2,1)S(1)} %get-tuple-element.98.refs_0_, bf16[256,384]{1,0:T(8,128)(2,1)S(1)} %last.3.refs_1_, bf16[256,512]{1,0:T(8,128)(2,1)S(1)} %collective-permute-done.16.refs_2_, ...), custom_call_target="tpu_custom_call" | custom-call | flops 822083584 | bytes 3211264 | tf_op jit(solution)/shard_map/project/pallas_call | solution.py:546
  82.6 5.5 %collective-permute-done.15.refs_0_ = bf16[256,384]{1,0:T(8,128)(2,1)S(1)} collective-permute-done((bf16[256,384]{1,0:T(8,128)(2,1)S(1)}, bf16[256,384]{1,0:T(8,128)(2,1)S(1)}, u32[]{:S(2)}, u32[]{:S(2)}) %collective-permute-start.15) | collective-permute-done | bytes 196640 | tf_op jit(solution)/shard_map/ppermute | solution.py:62
  88.1 0.0 collective-permute-done.14.refs_0_
  88.1 1.3 %collective-permute-start.19 = (bf16[256,512]{1,0:T(8,128)(2,1)S(1)}, bf16[256,512]{1,0:T(8,128)(2,1)S(1)}, u32[]{:S(2)}, u32[]{:S(2)}) collective-permute-start(bf16[256,512]{1,0:T(8,128)(2,1)S(1)} %collective-permute-done.14.refs_0_), channel_id=1, source_target_pairs={{0,1},{1,0},{2,3},{3,2},{4,5},{5,4},{6,7},{7,6},{8,9},{9,8},{10,11... | collective-permute-start | bytes 786440 | tf_op jit(solution)/shard_map/ppermute | solution.py:62
  89.4 0.0 collective-permute-start.18
  89.4 1.2 %collective-permute-done.19.refs_1_ = bf16[256,512]{1,0:T(8,128)(2,1)S(1)} collective-permute-done((bf16[256,512]{1,0:T(8,128)(2,1)S(1)}, bf16[256,512]{1,0:T(8,128)(2,1)S(1)}, u32[]{:S(2)}, u32[]{:S(2)}) %collective-permute-start.19) | collective-permute-done | bytes 262176 | tf_op jit(solution)/shard_map/ppermute | solution.py:62
  90.5 1.3 %project.4.refs_2_ = f32[256,896]{1,0:T(8,128)S(1)} custom-call(s32[4]{0:T(128)S(1)} %pad_add_fusion.groups, bf16[3584,896]{1,0:T(8,128)(2,1)S(1)} %copy-done, bf16[256,512]{1,0:T(8,128)(2,1)S(1)} %collective-permute-done.14.refs_0_, bf16[256,512]{1,0:T(8,128)(2,1)S(1)} %collective-permute-done.19.refs_1_, f32[256,896]{1,0:T(8,128)S(1)} %project.3.refs_2_), custom_call_target="tpu_custom_call" | custom-call | flops 469762048 | bytes 1835008 | tf_op jit(solution)/shard_map/project/pallas_call | solution.py:546
  91.8 0.0 collective-permute-done.18.refs_1_
  91.8 2.0 %project.5 = bf16[256,896]{1,0:T(8,128)(2,1)} custom-call(s32[4]{0:T(128)S(1)} %pad_add_fusion.groups, bf16[3584,896]{1,0:T(8,128)(2,1)S(1)} %copy-done, bf16[256,384]{1,0:T(8,128)(2,1)S(1)} %collective-permute-done.15.refs_0_, bf16[256,384]{1,0:T(8,128)(2,1)S(1)} %collective-permute-done.18.refs_1_, f32[256,896]{1,0:T(8,128)S(1)} %project.4.refs_2_), custom_call_target="tpu_custom_call" | custom-call | flops 352321536 | bytes 1376256 | tf_op jit(solution)/shard_map/project/pallas_call | solution.py:546
  (27 shorter events, 0.0 us)
Async XLA Ops:
  1.5 10.6 %collective-permute-start.10 = (bf16[256,256]{1,0:T(8,128)(2,1)}, bf16[256,256]{1,0:T(8,128)(2,1)S(1)}, u32[]{:S(2)}, u32[]{:S(2)}) collective-permute-start(bf16[256,256]{1,0:T(8,128)(2,1)} %join.1.refs_0_.refs_2_.refs_1_), channel_id=1, source_target_pairs={{0,12},{64,116},{4,16},{68,120},{8,20},{72,124},{12,24},{76,64},{1... | collective-permute-start | bytes 393224 | tf_op jit(solution)/shard_map/ppermute | solution.py:58
  4.1 8.1 %collective-permute-start.9 = (bf16[256,256]{1,0:T(8,128)(2,1)}, bf16[256,256]{1,0:T(8,128)(2,1)S(1)}, u32[]{:S(2)}, u32[]{:S(2)}) collective-permute-start(bf16[256,256]{1,0:T(8,128)(2,1)} %join.1.refs_0_.refs_2_.refs_1_), channel_id=1, source_target_pairs={{0,8},{64,120},{4,12},{68,124},{8,16},{72,64},{12,20},{76,68},{16,... | collective-permute-start | bytes 393224 | tf_op jit(solution)/shard_map/ppermute | solution.py:58
  4.4 10.4 %collective-permute-start.4 = (bf16[256,256]{1,0:T(8,128)(2,1)}, bf16[256,256]{1,0:T(8,128)(2,1)S(1)}, u32[]{:S(2)}, u32[]{:S(2)}) collective-permute-start(bf16[256,256]{1,0:T(8,128)(2,1)} %join.1.refs_0_.refs_2_.refs_1_), channel_id=1, source_target_pairs={{0,64},{64,0},{1,65},{65,1},{2,66},{66,2},{3,67},{67,3},{4,68},{68... | collective-permute-start | bytes 393224 | tf_op jit(solution)/shard_map/ppermute | solution.py:62
  8.9 6.2 %collective-permute-start.8 = (bf16[256,256]{1,0:T(8,128)(2,1)}, bf16[256,256]{1,0:T(8,128)(2,1)S(1)}, u32[]{:S(2)}, u32[]{:S(2)}) collective-permute-start(bf16[256,256]{1,0:T(8,128)(2,1)} %join.1.refs_0_.refs_2_.refs_1_), channel_id=1, source_target_pairs={{0,4},{64,124},{4,8},{68,64},{8,12},{72,68},{12,16},{76,72},{16,20... | collective-permute-start | bytes 393224 | tf_op jit(solution)/shard_map/ppermute | solution.py:58
  8.9 7.2 %collective-permute-start.3 = (bf16[256,256]{1,0:T(8,128)(2,1)}, bf16[256,256]{1,0:T(8,128)(2,1)S(1)}, u32[]{:S(2)}, u32[]{:S(2)}) collective-permute-start(bf16[256,256]{1,0:T(8,128)(2,1)} %join.1.refs_0_.refs_2_.refs_1_), channel_id=1, source_target_pairs={{0,8},{1,33},{4,12},{5,37},{8,0},{9,41},{12,4},{13,45},{16,24},{17... | collective-permute-start | bytes 393224 | tf_op jit(solution)/shard_map/ppermute | solution.py:50
  12.2 14.1 %copy-start.11 = (bf16[256,256]{1,0:T(8,128)(2,1)}, bf16[256,256]{1,0:T(8,128)(2,1)S(1)}, u32[]{:S(2)}) copy-start(bf16[256,256]{1,0:T(8,128)(2,1)S(1)} %collective-permute-done.10.refs_10_.refs_5_) | copy-start | bytes 393220
  12.2 9.5 %collective-permute-start.2 = (bf16[256,256]{1,0:T(8,128)(2,1)}, bf16[256,256]{1,0:T(8,128)(2,1)S(1)}, u32[]{:S(2)}, u32[]{:S(2)}) collective-permute-start(bf16[256,256]{1,0:T(8,128)(2,1)} %join.1.refs_0_.refs_2_.refs_1_), channel_id=1, source_target_pairs={{0,12},{1,49},{4,0},{5,53},{8,4},{9,57},{12,8},{13,61},{16,28},{17... | collective-permute-start | bytes 393224 | tf_op jit(solution)/shard_map/ppermute | solution.py:50
  12.2 14.1 %copy-start.13 = (bf16[256,256]{1,0:T(8,128)(2,1)}, bf16[256,256]{1,0:T(8,128)(2,1)S(1)}, u32[]{:S(2)}) copy-start(bf16[256,256]{1,0:T(8,128)(2,1)S(1)} %collective-permute-done.9.refs_9_.refs_4_) | copy-start | bytes 393220
  12.2 9.4 %collective-permute-start.1 = (bf16[256,256]{1,0:T(8,128)(2,1)}, bf16[256,256]{1,0:T(8,128)(2,1)S(1)}, u32[]{:S(2)}, u32[]{:S(2)}) collective-permute-start(bf16[256,256]{1,0:T(8,128)(2,1)} %join.1.refs_0_.refs_2_.refs_1_), channel_id=1, source_target_pairs={{0,4},{1,17},{4,8},{5,21},{8,12},{9,25},{12,0},{13,29},{16,20},{17... | collective-permute-start | bytes 393224 | tf_op jit(solution)/shard_map/ppermute | solution.py:50
  14.9 6.8 %collective-permute-start.7 = (bf16[256,256]{1,0:T(8,128)(2,1)S(1)}, bf16[256,256]{1,0:T(8,128)(2,1)S(1)}, u32[]{:S(2)}, u32[]{:S(2)}) collective-permute-start(bf16[256,256]{1,0:T(8,128)(2,1)S(1)} %collective-permute-done.4.refs_4_), channel_id=1, source_target_pairs={{0,8},{1,33},{4,12},{5,37},{8,0},{9,41},{12,4},{13,45},{16,24},{17... | collective-permute-start | bytes 393224 | tf_op jit(solution)/shard_map/ppermute | solution.py:50
  15.2 12.0 %copy-start.15 = (bf16[256,256]{1,0:T(8,128)(2,1)}, bf16[256,256]{1,0:T(8,128)(2,1)S(1)}, u32[]{:S(2)}) copy-start(bf16[256,256]{1,0:T(8,128)(2,1)S(1)} %collective-permute-done.8.refs_8_.refs_3_) | copy-start | bytes 393220
  15.2 8.2 %collective-permute-start.6 = (bf16[256,256]{1,0:T(8,128)(2,1)S(1)}, bf16[256,256]{1,0:T(8,128)(2,1)S(1)}, u32[]{:S(2)}, u32[]{:S(2)}) collective-permute-start(bf16[256,256]{1,0:T(8,128)(2,1)S(1)} %collective-permute-done.4.refs_4_), channel_id=1, source_target_pairs={{0,12},{1,49},{4,0},{5,53},{8,4},{9,57},{12,8},{13,61},{16,28},{17... | collective-permute-start | bytes 393224 | tf_op jit(solution)/shard_map/ppermute | solution.py:50
  16.2 10.2 %copy-start.5 = (bf16[256,256]{1,0:T(8,128)(2,1)}, bf16[256,256]{1,0:T(8,128)(2,1)S(1)}, u32[]{:S(2)}) copy-start(bf16[256,256]{1,0:T(8,128)(2,1)S(1)} %collective-permute-done.3.refs_3_.refs_4_) | copy-start | bytes 393220
  16.2 7.2 %collective-permute-start.5 = (bf16[256,256]{1,0:T(8,128)(2,1)S(1)}, bf16[256,256]{1,0:T(8,128)(2,1)S(1)}, u32[]{:S(2)}, u32[]{:S(2)}) collective-permute-start(bf16[256,256]{1,0:T(8,128)(2,1)S(1)} %collective-permute-done.4.refs_4_), channel_id=1, source_target_pairs={{0,4},{1,17},{4,8},{5,21},{8,12},{9,25},{12,0},{13,29},{16,20},{17... | collective-permute-start | bytes 393224 | tf_op jit(solution)/shard_map/ppermute | solution.py:50
  21.6 4.7 %copy-start.7 = (bf16[256,256]{1,0:T(8,128)(2,1)}, bf16[256,256]{1,0:T(8,128)(2,1)S(1)}, u32[]{:S(2)}) copy-start(bf16[256,256]{1,0:T(8,128)(2,1)S(1)} %collective-permute-done.2.refs_2_.refs_3_) | copy-start | bytes 393220
  21.6 4.7 %copy-start.9 = (bf16[256,256]{1,0:T(8,128)(2,1)}, bf16[256,256]{1,0:T(8,128)(2,1)S(1)}, u32[]{:S(2)}) copy-start(bf16[256,256]{1,0:T(8,128)(2,1)S(1)} %collective-permute-done.1.refs_1_.refs_2_) | copy-start | bytes 393220
  23.4 22.1 %slice-start = ((s8[6422528]{0:T(1024)(128)(4,1)}), s8[2228224]{0:T(1024)(128)(4,1)S(1)}, s32[]{:S(2)}) async-start(s8[6422528]{0:T(1024)(128)(4,1)} %bitcast.9), calls=%async_computation | async-start | bytes 4456448
  26.4 0.9 copy-start.1
  27.2 18.3 %collective-permute-start.11 = (bf16[1280,256]{1,0:T(8,128)(2,1)}, bf16[1280,256]{1,0:T(8,128)(2,1)S(1)}, u32[]{:S(2)}, u32[]{:S(2)}) collective-permute-start(bf16[1280,256]{1,0:T(8,128)(2,1)} %get-tuple-element.90), channel_id=1, source_target_pairs={{0,16},{1,5},{4,20},{5,9},{8,24},{9,13},{12,28},{13,1},{16,32},{17... | collective-permute-start | bytes 1966088 | tf_op jit(solution)/shard_map/ppermute | solution.py:50
  27.2 18.3 %collective-permute-start.12 = (bf16[1280,256]{1,0:T(8,128)(2,1)}, bf16[1280,256]{1,0:T(8,128)(2,1)S(1)}, u32[]{:S(2)}, u32[]{:S(2)}) collective-permute-start(bf16[1280,256]{1,0:T(8,128)(2,1)} %get-tuple-element.91), channel_id=1, source_target_pairs={{0,48},{1,13},{4,52},{5,1},{8,56},{9,5},{12,60},{13,9},{16,0},{17,... | collective-permute-start | bytes 1966088 | tf_op jit(solution)/shard_map/ppermute | solution.py:50
  29.9 27.9 %collective-permute-start.13 = (bf16[1280,256]{1,0:T(8,128)(2,1)}, bf16[1280,256]{1,0:T(8,128)(2,1)}, u32[]{:S(2)}, u32[]{:S(2)}) collective-permute-start(bf16[1280,256]{1,0:T(8,128)(2,1)} %get-tuple-element.92), channel_id=1, source_target_pairs={{0,32},{1,9},{4,36},{5,13},{8,40},{9,1},{12,44},{13,5},{16,48},{17... | collective-permute-start | bytes 1966088 | tf_op jit(solution)/shard_map/ppermute | solution.py:50
  31.6 1.1 %copy-start.2 = (bf16[1280,256]{1,0:T(8,128)(2,1)S(1)}, bf16[1280,256]{1,0:T(8,128)(2,1)}, u32[]{:S(2)}) copy-start(bf16[1280,256]{1,0:T(8,128)(2,1)} %copy-done.1) | copy-start | bytes 1966084
  32.7 1.0 %copy-start.4 = (bf16[256,896]{1,0:T(8,128)(2,1)S(1)}, bf16[256,896]{1,0:T(8,128)(2,1)}, u32[]{:S(2)}) copy-start(bf16[256,896]{1,0:T(8,128)(2,1)} %refs_0_.1) | copy-start | bytes 1376260
  33.7 7.0 %copy-start.12 = (bf16[256,256]{1,0:T(8,128)(2,1)S(1)}, bf16[256,256]{1,0:T(8,128)(2,1)}, u32[]{:S(2)}) copy-start(bf16[256,256]{1,0:T(8,128)(2,1)} %copy-done.11) | copy-start | bytes 393220
  33.7 7.0 %copy-start.14 = (bf16[256,256]{1,0:T(8,128)(2,1)S(1)}, bf16[256,256]{1,0:T(8,128)(2,1)}, u32[]{:S(2)}) copy-start(bf16[256,256]{1,0:T(8,128)(2,1)} %copy-done.13) | copy-start | bytes 393220
  33.7 7.0 %copy-start.16 = (bf16[256,256]{1,0:T(8,128)(2,1)S(1)}, bf16[256,256]{1,0:T(8,128)(2,1)}, u32[]{:S(2)}) copy-start(bf16[256,256]{1,0:T(8,128)(2,1)} %copy-done.15) | copy-start | bytes 393220
  33.7 11.8 %slice-start.1 = ((s8[6422528]{0:T(1024)(128)(4,1)}), s8[4194304]{0:T(1024)(128)(4,1)S(1)}, s32[]{:S(2)}) async-start(s8[6422528]{0:T(1024)(128)(4,1)} %bitcast.9), calls=%async_computation.1 | async-start | bytes 8388608
  45.5 12.3 %copy-start.3 = (bf16[1280,256]{1,0:T(8,128)(2,1)S(1)}, bf16[1280,256]{1,0:T(8,128)(2,1)}, u32[]{:S(2)}) copy-start(bf16[1280,256]{1,0:T(8,128)(2,1)} %copy-done.1) | copy-start | bytes 1966084
  45.5 12.3 %copy-start.6 = (bf16[256,256]{1,0:T(8,128)(2,1)S(1)}, bf16[256,256]{1,0:T(8,128)(2,1)}, u32[]{:S(2)}) copy-start(bf16[256,256]{1,0:T(8,128)(2,1)} %copy-done.5) | copy-start | bytes 393220
  45.5 12.3 %copy-start.8 = (bf16[256,256]{1,0:T(8,128)(2,1)S(1)}, bf16[256,256]{1,0:T(8,128)(2,1)}, u32[]{:S(2)}) copy-start(bf16[256,256]{1,0:T(8,128)(2,1)} %copy-done.7) | copy-start | bytes 393220
  45.6 12.3 %copy-start.10 = (bf16[256,256]{1,0:T(8,128)(2,1)S(1)}, bf16[256,256]{1,0:T(8,128)(2,1)}, u32[]{:S(2)}) copy-start(bf16[256,256]{1,0:T(8,128)(2,1)} %copy-done.9) | copy-start | bytes 393220
  64.3 13.6 %collective-permute-start.16 = (bf16[256,512]{1,0:T(8,128)(2,1)S(1)}, bf16[256,512]{1,0:T(8,128)(2,1)S(1)}, u32[]{:S(2)}, u32[]{:S(2)}) collective-permute-start(bf16[256,512]{1,0:T(8,128)(2,1)S(1)} %get-tuple-element.98.refs_0_), channel_id=1, source_target_pairs={{0,1},{1,0},{2,3},{3,2},{4,5},{5,4},{6,7},{7,6},{8,9},{9,8},{10,11... | collective-permute-start | bytes 786440 | tf_op jit(solution)/shard_map/ppermute | solution.py:62
  76.3 1.7 %collective-permute-start.17 = (bf16[256,384]{1,0:T(8,128)(2,1)S(1)}, bf16[256,384]{1,0:T(8,128)(2,1)S(1)}, u32[]{:S(2)}, u32[]{:S(2)}) collective-permute-start(bf16[256,384]{1,0:T(8,128)(2,1)S(1)} %last.3.refs_1_), channel_id=1, source_target_pairs={{0,1},{1,0},{2,3},{3,2},{4,5},{5,4},{6,7},{7,6},{8,9},{9,8},{10,11... | collective-permute-start | bytes 589832 | tf_op jit(solution)/shard_map/ppermute | solution.py:62
  76.4 11.8 %collective-permute-start.14 = (bf16[256,512]{1,0:T(8,128)(2,1)S(1)}, bf16[256,512]{1,0:T(8,128)(2,1)S(1)}, u32[]{:S(2)}, u32[]{:S(2)}) collective-permute-start(bf16[256,512]{1,0:T(8,128)(2,1)S(1)} %get-tuple-element.98.refs_0_), channel_id=1, source_target_pairs={{0,2},{2,0},{1,3},{3,1},{4,6},{6,4},{5,7},{7,5},{8,10},{10,8},{9,1... | collective-permute-start | bytes 786440 | tf_op jit(solution)/shard_map/ppermute | solution.py:62
  77.1 11.0 %collective-permute-start.15 = (bf16[256,384]{1,0:T(8,128)(2,1)S(1)}, bf16[256,384]{1,0:T(8,128)(2,1)S(1)}, u32[]{:S(2)}, u32[]{:S(2)}) collective-permute-start(bf16[256,384]{1,0:T(8,128)(2,1)S(1)} %last.3.refs_1_), channel_id=1, source_target_pairs={{0,2},{2,0},{1,3},{3,1},{4,6},{6,4},{5,7},{7,5},{8,10},{10,8},{9,1... | collective-permute-start | bytes 589832 | tf_op jit(solution)/shard_map/ppermute | solution.py:62
  78.0 2.8 %copy-start = (bf16[3584,896]{1,0:T(8,128)(2,1)S(1)}, bf16[3584,896]{1,0:T(8,128)(2,1)}, u32[]{:S(2)}) copy-start(bf16[3584,896]{1,0:T(8,128)(2,1)} %weight.5) | copy-start | bytes 19267588
  88.1 2.4 %collective-permute-start.19 = (bf16[256,512]{1,0:T(8,128)(2,1)S(1)}, bf16[256,512]{1,0:T(8,128)(2,1)S(1)}, u32[]{:S(2)}, u32[]{:S(2)}) collective-permute-start(bf16[256,512]{1,0:T(8,128)(2,1)S(1)} %collective-permute-done.14.refs_0_), channel_id=1, source_target_pairs={{0,1},{1,0},{2,3},{3,2},{4,5},{5,4},{6,7},{7,6},{8,9},{9,8},{10,11... | collective-permute-start | bytes 786440 | tf_op jit(solution)/shard_map/ppermute | solution.py:62
  89.4 2.4 %collective-permute-start.18 = (bf16[256,384]{1,0:T(8,128)(2,1)S(1)}, bf16[256,384]{1,0:T(8,128)(2,1)S(1)}, u32[]{:S(2)}, u32[]{:S(2)}) collective-permute-start(bf16[256,384]{1,0:T(8,128)(2,1)S(1)} %collective-permute-done.15.refs_0_), channel_id=1, source_target_pairs={{0,1},{1,0},{2,3},{3,2},{4,5},{5,4},{6,7},{7,6},{8,9},{9,8},{10,11... | collective-permute-start | bytes 589832 | tf_op jit(solution)/shard_map/ppermute | solution.py:62

commit v3 on v2

--- a/solution.py
+++ b/solution.py
@@ -477,21 +477,21 @@
     )(table, queries, own)
 
 
-def attend_middle(table, rows, messages, state, weight, after):
+def attend_middle(table, rows, messages, state, after):
     def kernel(*refs):
-        middle_kernel(*refs[:6], *refs[8:])
+        middle_kernel(*refs[:6], *refs[7:])
 
     return pl.pallas_call(
         kernel,
         out_shape=STATE,
-        in_specs=[SMEM] + [VMEM] * 6 + [HBM],
+        in_specs=[SMEM] + [VMEM] * 5 + [HBM],
         out_specs=[VMEM] * 2,
         scratch_shapes=scratch(2 * PIECE),
         input_output_aliases={4: 0, 5: 1},
         compiler_params=PARAMS,
         cost_estimate=cost(2 * PIECE),
         name="middle",
-    )(table, rows, *messages, *state, weight, after)
+    )(table, rows, *messages, *state, after)
 
 
 def attend_last(low, high, table, blocks, more):
@@ -534,26 +534,42 @@
     return total
 
 
-def project_kernel(where, groups, weight, *refs):
-    parts, before, out = refs[:len(where)], refs[len(where):-1], refs[-1]
-    total = before[0][...] if before else None
-    total = add_products(total, groups, weight, [(*w, p) for w, p in zip(where, parts)])
+def near_kernel(where, groups, weight, *refs):
+    parts, (out, held, sem) = refs[:len(where)], refs[len(where):]
+    copy = pltpu.make_async_copy(weight, held, sem)
+    copy.start()
+    copy.wait()
+    out[...] = add_products(None, groups, held, [(*w, p) for w, p in zip(where, parts)])
+
+
+def rest_kernel(where, groups, weight, *refs):
+    parts, (before, out) = refs[:len(where)], refs[len(where):]
+    total = add_products(before[...], groups, weight, [(*w, p) for w, p in zip(where, parts)])
     out[...] = total.astype(out.dtype)
 
 
-def project(where, groups, weight, parts, before, dtype):
+def project(where, groups, weight, parts, before=None):
     depth = sum(part.shape[1] for part in parts)
+    shape = (TOK, weight.shape[1])
+    if before is None:
+        kernel, operands, place, scratches = near_kernel, parts, HBM, [pltpu.SemaphoreType.DMA]
+        out_shape = [
+            jax.ShapeDtypeStruct(shape, jnp.float32), jax.ShapeDtypeStruct(weight.shape, weight.dtype)]
+    else:
+        kernel, operands, place, scratches = rest_kernel, [*parts, before], VMEM, []
+        out_shape = [jax.ShapeDtypeStruct(shape, jnp.bfloat16)]
     return pl.pallas_call(
-        functools.partial(project_kernel, where),
-        out_shape=jax.ShapeDtypeStruct((TOK, weight.shape[1]), dtype),
-        in_specs=[SMEM] + [VMEM] * (1 + len(parts) + len(before)),
-        out_specs=VMEM,
-        compiler_params=pltpu.CompilerParams(vmem_limit_bytes=20 * 2**20),
+        functools.partial(kernel, where),
+        out_shape=out_shape,
+        in_specs=[SMEM, place] + [VMEM] * len(operands),
+        out_specs=[VMEM] * len(out_shape),
+        scratch_shapes=scratches,
+        compiler_params=pltpu.CompilerParams(vmem_limit_bytes=12 * 2**20),
         cost_estimate=pl.CostEstimate(
             flops=2 * TOK * depth * weight.shape[1], bytes_accessed=2 * depth * weight.shape[1],
             transcendentals=0),
         name="project",
-    )(groups, weight, *parts, *before)
+    )(groups, weight, *operands)
 
 
 def per_device(queries, keys, values, doc_lengths, out_weight):
@@ -580,7 +596,7 @@
     beyond_rings = lax.cond(is_far[0] == 1, fetch, lambda block: nothing, native)
     rows, *state = attend_own(table, queries, own)
     small = attend_small((table, is_far), (queries, native, *rings, beyond_rings, rows))
-    state = attend_middle(table, rows, messages[:2], state, out_weight, small)
+    state = attend_middle(table, rows, messages[:2], state, small)
     (first, middle), (second, _) = CHUNKS
     some, rest = attend_last(
         first, middle, table, (rows, own, *messages, small, *state), (queries, *natives))
@@ -590,16 +606,13 @@
     beside = [swap(part, "c") for part in chunks]
     group = (zl * 2 + c).astype(jnp.int32)
     groups = jnp.stack([group, group ^ 1, group ^ 2, group ^ 3])
-    mixed = project(
-        [(0, first), (0, second), (1, first), (1, second)], groups, out_weight, chunks + beside, [],
-        jnp.float32)
+    mixed, weight = project(
+        [(0, first), (0, second), (1, first), (1, second)], groups, out_weight, chunks + beside)
     across, mixed = lax.optimization_barrier((across, mixed))
     beyond = [swap(part, "c") for part in across]
-    mixed = project(
-        [(2, first), (3, first)], groups, out_weight, [across[0], beyond[0]], [mixed], jnp.float32)
     return project(
-        [(2, second), (3, second)], groups, out_weight, [across[1], beyond[1]], [mixed],
-        jnp.bfloat16)
+        [(2, first), (3, first), (2, second), (3, second)], groups, weight,
+        [across[0], beyond[0], across[1], beyond[1]], mixed)[0]
 
 
 def solution(mesh):

time: 94.2 us -> 90.9 us (0.965)
  local copies, waits for them, and re-layouts: 7.68 us -> 4.72 us
  Pallas kernels: 42.2 us -> 40 us
  waiting for transfers between devices: 11.6 us -> 13.7 us
    unnamed x38 -> x22, local copies, waits for them, and re-layouts: 5.84 us -> 2.87 us
    ppermute x9, waiting for transfers between devices: 4.59 us -> 7.44 us  [move(): return lax.ppermute(block, ('y', 'x', 'c'), turn(by_first, by_second))]
    pallas_call x4 -> x3, Pallas kernels: 17.3 us -> 17.5 us  [the longest x1 12.1 us: attend_middle(): pl.pallas_call(kernel, out_shape=STATE, in_specs=[SMEM] + [VMEM] * 5 + [H...]
  transfers between devices with their start and end apart: 19 -> 19, of which waited for: 5 -> 5; matrix products, arithmetic and copies ran while one was open for 2% -> 2% of each run, Pallas kernels for 31% -> 30%
where the time goes in v3:
time: 90.9 us; the launch traced here: 90.7 us
  Pallas kernels  40 us (44%)
  starting transfers between devices  31.4 us (35%)
  waiting for transfers between devices  13.7 us (15%)
  local copies, waits for them, and re-layouts  4.72 us (5%)
    ppermute x9, starting transfers between devices, move(): return lax.ppermute(block, ('y', 'x', 'c'), turn(by_first, by_second))  14.3 us
    ppermute x7, starting transfers between devices, swap(): return lax.ppermute(block, axis, [(0, 1), (1, 0)])  14.2 us
    pallas_call x1, Pallas kernels, attend_middle(): pl.pallas_call(kernel, out_shape=STATE, in_specs=[SMEM] + [VMEM] * 5 + [H...  12.1 us
    pallas_call x2, Pallas kernels, attend_last(): pl.pallas_call(functools.partial(last_kernel, low, high), out_shape=shape...  11.2 us
    ppermute x9, waiting for transfers between devices, move(): return lax.ppermute(block, ('y', 'x', 'c'), turn(by_first, by_second))  7.44 us
    pallas_call x1, Pallas kernels, attend_own(): pl.pallas_call(own_kernel, out_shape=[rows] + STATE, in_specs=[SMEM, VMEM...  6.92 us
    ppermute x7, waiting for transfers between devices, swap(): return lax.ppermute(block, axis, [(0, 1), (1, 0)])  6.15 us
    pallas_call x2, Pallas kernels, project(): pl.pallas_call(functools.partial(kernel, where), out_shape=out_shape, in_...  5.36 us
  transfers between devices with their start and end apart: 19, of which 5 were waited for; matrix products, arithmetic and copies ran while one was open for 2% of the time, Pallas kernels for 30%

profile of v3, /device:TPU:25, one launch (start us, length us, event | category | flops | bytes accessed | tf_op | source)
XLA Modules:
  0.0 90.7 jit_solution(6509081488182007576)
XLA Ops:
  0.0 0.9 join.1.refs_0_.refs_2_.refs_1_
  0.9 0.0 copy-start.9
  0.9 2.5 %collective-permute-start.10 = (bf16[256,256]{1,0:T(8,128)(2,1)S(1)}, bf16[256,256]{1,0:T(8,128)(2,1)S(1)}, u32[]{:S(2)}, u32[]{:S(2)}) collective-permute-start(bf16[256,256]{1,0:T(8,128)(2,1)S(1)} %join.1.refs_0_.refs_2_.refs_1_), channel_id=1, source_target_pairs={{0,12},{64,116},{4,16},{68,120},{8,20},{72,124},{12,24},{76,64},{1... | collective-permute-start | bytes 393224 | tf_op jit(solution)/shard_map/ppermute | solution.py:58
  3.5 0.3 collective-permute-start.9
  3.8 4.5 %collective-permute-start.4 = (bf16[256,256]{1,0:T(8,128)(2,1)S(1)}, bf16[256,256]{1,0:T(8,128)(2,1)S(1)}, u32[]{:S(2)}, u32[]{:S(2)}) collective-permute-start(bf16[256,256]{1,0:T(8,128)(2,1)S(1)} %join.1.refs_0_.refs_2_.refs_1_), channel_id=1, source_target_pairs={{0,64},{64,0},{1,65},{65,1},{2,66},{66,2},{3,67},{67,3},{4,68},{68... | collective-permute-start | bytes 393224 | tf_op jit(solution)/shard_map/ppermute | solution.py:62
  8.3 0.0 collective-permute-start.8
  8.3 3.2 %collective-permute-start.3 = (bf16[256,256]{1,0:T(8,128)(2,1)S(1)}, bf16[256,256]{1,0:T(8,128)(2,1)S(1)}, u32[]{:S(2)}, u32[]{:S(2)}) collective-permute-start(bf16[256,256]{1,0:T(8,128)(2,1)S(1)} %join.1.refs_0_.refs_2_.refs_1_), channel_id=1, source_target_pairs={{0,8},{1,33},{4,12},{5,37},{8,0},{9,41},{12,4},{13,45},{16,24},{17... | collective-permute-start | bytes 393224 | tf_op jit(solution)/shard_map/ppermute | solution.py:50
  11.5 0.0 collective-permute-done.10.refs_10_.refs_5_
  11.5 0.0 collective-permute-start.2
  11.5 0.0 collective-permute-done.9.refs_9_.refs_4_
  11.6 0.0 copy-start.4
  11.6 2.7 %collective-permute-start.1 = (bf16[256,256]{1,0:T(8,128)(2,1)S(1)}, bf16[256,256]{1,0:T(8,128)(2,1)S(1)}, u32[]{:S(2)}, u32[]{:S(2)}) collective-permute-start(bf16[256,256]{1,0:T(8,128)(2,1)S(1)} %join.1.refs_0_.refs_2_.refs_1_), channel_id=1, source_target_pairs={{0,4},{1,17},{4,8},{5,21},{8,12},{9,25},{12,0},{13,29},{16,20},{17... | collective-permute-start | bytes 393224 | tf_op jit(solution)/shard_map/ppermute | solution.py:50
  14.2 0.0 collective-permute-done.4.refs_4_
  14.2 0.0 collective-permute-start.7
  14.2 0.1 collective-permute-done.8.refs_8_.refs_3_
  14.3 1.0 %collective-permute-start.6 = (bf16[256,256]{1,0:T(8,128)(2,1)S(1)}, bf16[256,256]{1,0:T(8,128)(2,1)S(1)}, u32[]{:S(2)}, u32[]{:S(2)}) collective-permute-start(bf16[256,256]{1,0:T(8,128)(2,1)S(1)} %collective-permute-done.4.refs_4_), channel_id=1, source_target_pairs={{0,12},{1,49},{4,0},{5,53},{8,4},{9,57},{12,8},{13,61},{16,28},{17... | collective-permute-start | bytes 393224 | tf_op jit(solution)/shard_map/ppermute | solution.py:50
  15.3 0.0 collective-permute-done.3.refs_3_.refs_4_
  15.3 4.7 %collective-permute-start.5 = (bf16[256,256]{1,0:T(8,128)(2,1)S(1)}, bf16[256,256]{1,0:T(8,128)(2,1)S(1)}, u32[]{:S(2)}, u32[]{:S(2)}) collective-permute-start(bf16[256,256]{1,0:T(8,128)(2,1)S(1)} %collective-permute-done.4.refs_4_), channel_id=1, source_target_pairs={{0,4},{1,17},{4,8},{5,21},{8,12},{9,25},{12,0},{13,29},{16,20},{17... | collective-permute-start | bytes 393224 | tf_op jit(solution)/shard_map/ppermute | solution.py:50
  20.0 0.7 concatenate.3.table.refs_0_
  20.8 0.0 collective-permute-done.2.refs_2_.refs_3_
  20.8 0.0 collective-permute-done.1.refs_1_.refs_2_
  20.8 0.0 collective-permute-done.7.refs_7_
  20.8 1.8 %collective-permute-done.6.refs_6_ = bf16[256,256]{1,0:T(8,128)(2,1)S(1)} collective-permute-done((bf16[256,256]{1,0:T(8,128)(2,1)S(1)}, bf16[256,256]{1,0:T(8,128)(2,1)S(1)}, u32[]{:S(2)}, u32[]{:S(2)}) %collective-permute-start.6) | collective-permute-done | bytes 131104 | tf_op jit(solution)/shard_map/ppermute | solution.py:50
  22.6 0.0 collective-permute-done.5.refs_5_
  22.6 2.4 %pack.1 = (bf16[1280,256]{1,0:T(8,128)(2,1)S(1)}, bf16[1280,256]{1,0:T(8,128)(2,1)}, bf16[1280,256]{1,0:T(8,128)(2,1)}, bf16[1280,256]{1,0:T(8,128)(2,1)}, s32[1]{0:T(128)}) custom-call(s32[20]{0:T(128)S(1)} %concatenate.3.table.refs_0_, bf16[256,256]{1,0:T(8,128)(2,1)S(1)} %join.1.refs_0_.refs_2_.refs_1_, ...), custom_call_target="tpu_custom_call" | custom-call | tf_op jit(solution)/shard_map/pack/pallas_call | solution.py:182
  25.0 0.0 copy-done.2
  25.0 0.0 copy-done.4
  25.0 0.0 copy-done.6
  25.0 0.1 collective-permute-start.11
  25.1 2.7 %collective-permute-start.12 = (bf16[1280,256]{1,0:T(8,128)(2,1)}, bf16[1280,256]{1,0:T(8,128)(2,1)S(1)}, u32[]{:S(2)}, u32[]{:S(2)}) collective-permute-start(bf16[1280,256]{1,0:T(8,128)(2,1)} %get-tuple-element.93), channel_id=1, source_target_pairs={{0,48},{1,13},{4,52},{5,1},{8,56},{9,5},{12,60},{13,9},{16,0},{17,... | collective-permute-start | bytes 1966088 | tf_op jit(solution)/shard_map/ppermute | solution.py:50
  27.7 0.0 collective-permute-start.13
  28.3 0.0 copy-start.1
  28.3 1.1 %conditional.1 = (bf16[2304,256]{1,0:T(8,128)(2,1)}) conditional(s32[]{:T(128)} %bitcast.8, () %tuple.26, bf16[256,256]{1,0:T(8,128)(2,1)} %copy-done.9), branch_computations={%region_0.0_spmd, %region_1.0_spmd} | conditional | flops 8 | bytes 2490649 | solution.py:596
  28.3 1.1 %broadcast_in_dim.4 = bf16[2304,256]{1,0:T(8,128)(2,1)} broadcast(bf16[]{:T(256)} %constant.50.clone), dimensions={} | broadcast | bytes 1179650 | tf_op jit(solution)/shard_map/broadcast_in_dim | solution.py:585
  29.5 0.0 copy-start.10
  29.5 6.9 %own.1 = (bf16[1792,128]{1,0:T(8,128)(2,1)S(1)}, f32[1800,128]{1,0:T(8,128)S(1)}, f32[1792,256]{1,0:T(8,128)S(1)}) custom-call(s32[20]{0:T(128)S(1)} %concatenate.3.table.refs_0_, bf16[256,896]{1,0:T(8,128)(2,1)S(1)} %copy-done.1, bf16[1280,256]{1,0:T(8,128)(2,1)S(1)} %get-tuple-element.90.own), custom_call_target="tpu_custom_call" | custom-call | flops 1409286144 | bytes 917504 | tf_op jit(solution)/shard_map/own/pallas_call | solution.py:468
  36.4 0.0 copy-done.3
  36.4 0.0 copy-done.5
  36.4 0.0 copy-done.7
  36.4 0.0 copy-done.8
  36.4 0.0 copy-done.10
  36.4 1.1 %small.1.refs_6_ = bf16[256,896]{1,0:T(8,128)(2,1)S(1)} custom-call(s32[20]{0:T(128)S(1)} %concatenate.3.table.refs_0_, s32[1]{0:T(128)} %get-tuple-element.95.refs_0_, bf16[256,896]{1,0:T(8,128)(2,1)S(1)} %copy-done.1, bf16[256,256]{1,0:T(8,128)(2,1)S(1)} %copy-done.10, bf16[256,256]{1,0:T(8,128)(2,1)S(1)} %copy-done.7, bf16[256,256]{1,0:T(8,128)(2,1)S(1)} %copy-done.5, ...), custom_call_target="tpu_custom_call" | custom-call | flops 352321536 | bytes 917504 | tf_op jit(solution)/shard_map/small/pallas_call | solution.py:517
  37.6 5.7 %collective-permute-done.11.refs_2_.b1 = bf16[1280,256]{1,0:T(8,128)(2,1)S(1)} collective-permute-done((bf16[1280,256]{1,0:T(8,128)(2,1)}, bf16[1280,256]{1,0:T(8,128)(2,1)S(1)}, u32[]{:S(2)}, u32[]{:S(2)}) %collective-permute-start.11) | collective-permute-done | bytes 655392 | tf_op jit(solution)/shard_map/ppermute | solution.py:50
  43.2 0.0 collective-permute-done.12.refs_3_.b2
  43.2 12.1 %middle.1 = (f32[1800,128]{1,0:T(8,128)S(1)}, f32[1792,256]{1,0:T(8,128)S(1)}) custom-call(s32[20]{0:T(128)S(1)} %concatenate.3.table.refs_0_, bf16[1792,128]{1,0:T(8,128)(2,1)S(1)} %get-tuple-element.91.refs_7_.refs_1_.rows_in, bf16[1280,256]{1,0:T(8,128)(2,1)S(1)} %collective-permute-done.11.refs_2_.b1, ...), custom_call_target="tpu_custom_call", output_to_operand_aliasing={{0}: (4, {}), {1}: (5, {})} | custom-call | flops 2818572288 | bytes 917504 | tf_op jit(solution)/shard_map/middle/pallas_call | solution.py:484
  55.4 0.0 collective-permute-done.13.b3
  55.4 6.6 %last.2 = (bf16[256,512]{1,0:T(8,128)(2,1)}, bf16[256,384]{1,0:T(8,128)(2,1)S(1)}) custom-call(s32[20]{0:T(128)S(1)} %concatenate.3.table.refs_0_, bf16[1792,128]{1,0:T(8,128)(2,1)S(1)} %get-tuple-element.91.refs_7_.refs_1_.rows_in, bf16[1280,256]{1,0:T(8,128)(2,1)S(1)} %get-tuple-element.90.own, bf16[1280,256]{1,0:T(8,128)(2,1)S(1)} %collective-permute-done.11.refs_2_.b1, ...), custom_call_target="tpu_custom_call" | custom-call | flops 1006632960 | bytes 524288 | tf_op jit(solution)/shard_map/last/pallas_call | solution.py:504
  62.0 6.8 %collective-permute-start.14 = (bf16[256,512]{1,0:T(8,128)(2,1)}, bf16[256,512]{1,0:T(8,128)(2,1)S(1)}, u32[]{:S(2)}, u32[]{:S(2)}) collective-permute-start(bf16[256,512]{1,0:T(8,128)(2,1)} %get-tuple-element.100.refs_0_), channel_id=1, source_target_pairs={{0,1},{1,0},{2,3},{3,2},{4,5},{5,4},{6,7},{7,6},{8,9},{9,8},{10,11... | collective-permute-start | bytes 786440 | tf_op jit(solution)/shard_map/ppermute | solution.py:62
  68.7 4.6 %last.3.refs_1_ = bf16[256,384]{1,0:T(8,128)(2,1)S(1)} custom-call(s32[20]{0:T(128)S(1)} %concatenate.3.table.refs_0_, bf16[1792,128]{1,0:T(8,128)(2,1)S(1)} %get-tuple-element.91.refs_7_.refs_1_.rows_in, bf16[1280,256]{1,0:T(8,128)(2,1)S(1)} %get-tuple-element.90.own, bf16[1280,256]{1,0:T(8,128)(2,1)S(1)} %collective-permute-done.11.refs_2_.b1, ...), custom_call_target="tpu_custom_call" | custom-call | flops 754974720 | bytes 393216 | tf_op jit(solution)/shard_map/last/pallas_call | solution.py:504
  73.3 0.1 collective-permute-start.15
  73.4 0.8 collective-permute-start.16
  74.2 0.8 collective-permute-start.17
  75.0 0.1 pad_add_fusion.groups
  75.1 0.0 collective-permute-done.15.refs_3_
  75.1 0.0 collective-permute-done.14.refs_2_
  75.1 2.8 %copy-done = bf16[3584,896]{1,0:T(8,128)(2,1)S(1)} copy-done((bf16[3584,896]{1,0:T(8,128)(2,1)S(1)}, bf16[3584,896]{1,0:T(8,128)(2,1)}, u32[]{:S(2)}) %copy-start) | copy-done | bytes 6422552
  77.9 2.8 %project.2 = (f32[256,896]{1,0:T(8,128)S(1)}, bf16[3584,896]{1,0:T(8,128)(2,1)S(1)}) custom-call(s32[4]{0:T(128)S(1)} %pad_add_fusion.groups, bf16[3584,896]{1,0:T(8,128)(2,1)S(1)} %copy-done, bf16[256,512]{1,0:T(8,128)(2,1)} %get-tuple-element.100.refs_0_, bf16[256,384]{1,0:T(8,128)(2,1)S(1)} %last.3.refs_1_, ...), custom_call_target="tpu_custom_call" | custom-call | flops 822083584 | bytes 3211264 | tf_op jit(solution)/shard_map/project/pallas_call | solution.py:561
  80.7 4.7 %collective-permute-done.17.refs_2_ = bf16[256,384]{1,0:T(8,128)(2,1)S(1)} collective-permute-done((bf16[256,384]{1,0:T(8,128)(2,1)S(1)}, bf16[256,384]{1,0:T(8,128)(2,1)S(1)}, u32[]{:S(2)}, u32[]{:S(2)}) %collective-permute-start.17) | collective-permute-done | bytes 196640 | tf_op jit(solution)/shard_map/ppermute | solution.py:62
  85.4 0.0 collective-permute-done.16.refs_0_
  85.4 1.3 %collective-permute-start.18 = (bf16[256,512]{1,0:T(8,128)(2,1)S(1)}, bf16[256,512]{1,0:T(8,128)(2,1)S(1)}, u32[]{:S(2)}, u32[]{:S(2)}) collective-permute-start(bf16[256,512]{1,0:T(8,128)(2,1)S(1)} %collective-permute-done.16.refs_0_), channel_id=1, source_target_pairs={{0,1},{1,0},{2,3},{3,2},{4,5},{5,4},{6,7},{7,6},{8,9},{9,8},{10,11... | collective-permute-start | bytes 786440 | tf_op jit(solution)/shard_map/ppermute | solution.py:62
  86.7 0.0 collective-permute-start.19
  86.7 1.4 %collective-permute-done.19.refs_3_ = bf16[256,384]{1,0:T(8,128)(2,1)S(1)} collective-permute-done((bf16[256,384]{1,0:T(8,128)(2,1)S(1)}, bf16[256,384]{1,0:T(8,128)(2,1)S(1)}, u32[]{:S(2)}, u32[]{:S(2)}) %collective-permute-start.19) | collective-permute-done | bytes 196640 | tf_op jit(solution)/shard_map/ppermute | solution.py:62
  88.1 0.0 collective-permute-done.18.refs_1_
  88.1 2.6 %project.3 = bf16[256,896]{1,0:T(8,128)(2,1)} custom-call(s32[4]{0:T(128)S(1)} %pad_add_fusion.groups, bf16[3584,896]{1,0:T(8,128)(2,1)S(1)} %get-tuple-element.102.weight, bf16[256,512]{1,0:T(8,128)(2,1)S(1)} %collective-permute-done.16.refs_0_, bf16[256,512]{1,0:T(8,128)(2,1)S(1)} %collective-permute-done.18.refs_1_, ...), custom_call_target="tpu_custom_call" | custom-call | flops 822083584 | bytes 3211264 | tf_op jit(solution)/shard_map/project/pallas_call | solution.py:561
  (9 shorter events, 0.0 us)
Async XLA Ops:
  0.9 24.2 %copy-start.9 = (bf16[256,256]{1,0:T(8,128)(2,1)}, bf16[256,256]{1,0:T(8,128)(2,1)S(1)}, u32[]{:S(2)}) copy-start(bf16[256,256]{1,0:T(8,128)(2,1)S(1)} %join.1.refs_0_.refs_2_.refs_1_) | copy-start | bytes 393220
  0.9 10.6 %collective-permute-start.10 = (bf16[256,256]{1,0:T(8,128)(2,1)S(1)}, bf16[256,256]{1,0:T(8,128)(2,1)S(1)}, u32[]{:S(2)}, u32[]{:S(2)}) collective-permute-start(bf16[256,256]{1,0:T(8,128)(2,1)S(1)} %join.1.refs_0_.refs_2_.refs_1_), channel_id=1, source_target_pairs={{0,12},{64,116},{4,16},{68,120},{8,20},{72,124},{12,24},{76,64},{1... | collective-permute-start | bytes 393224 | tf_op jit(solution)/shard_map/ppermute | solution.py:58
  3.5 8.1 %collective-permute-start.9 = (bf16[256,256]{1,0:T(8,128)(2,1)S(1)}, bf16[256,256]{1,0:T(8,128)(2,1)S(1)}, u32[]{:S(2)}, u32[]{:S(2)}) collective-permute-start(bf16[256,256]{1,0:T(8,128)(2,1)S(1)} %join.1.refs_0_.refs_2_.refs_1_), channel_id=1, source_target_pairs={{0,8},{64,120},{4,12},{68,124},{8,16},{72,64},{12,20},{76,68},{16,... | collective-permute-start | bytes 393224 | tf_op jit(solution)/shard_map/ppermute | solution.py:58
  3.8 10.4 %collective-permute-start.4 = (bf16[256,256]{1,0:T(8,128)(2,1)S(1)}, bf16[256,256]{1,0:T(8,128)(2,1)S(1)}, u32[]{:S(2)}, u32[]{:S(2)}) collective-permute-start(bf16[256,256]{1,0:T(8,128)(2,1)S(1)} %join.1.refs_0_.refs_2_.refs_1_), channel_id=1, source_target_pairs={{0,64},{64,0},{1,65},{65,1},{2,66},{66,2},{3,67},{67,3},{4,68},{68... | collective-permute-start | bytes 393224 | tf_op jit(solution)/shard_map/ppermute | solution.py:62
  8.3 6.0 %collective-permute-start.8 = (bf16[256,256]{1,0:T(8,128)(2,1)S(1)}, bf16[256,256]{1,0:T(8,128)(2,1)S(1)}, u32[]{:S(2)}, u32[]{:S(2)}) collective-permute-start(bf16[256,256]{1,0:T(8,128)(2,1)S(1)} %join.1.refs_0_.refs_2_.refs_1_), channel_id=1, source_target_pairs={{0,4},{64,124},{4,8},{68,64},{8,12},{72,68},{12,16},{76,72},{16,20... | collective-permute-start | bytes 393224 | tf_op jit(solution)/shard_map/ppermute | solution.py:58
  8.3 7.0 %collective-permute-start.3 = (bf16[256,256]{1,0:T(8,128)(2,1)S(1)}, bf16[256,256]{1,0:T(8,128)(2,1)S(1)}, u32[]{:S(2)}, u32[]{:S(2)}) collective-permute-start(bf16[256,256]{1,0:T(8,128)(2,1)S(1)} %join.1.refs_0_.refs_2_.refs_1_), channel_id=1, source_target_pairs={{0,8},{1,33},{4,12},{5,37},{8,0},{9,41},{12,4},{13,45},{16,24},{17... | collective-permute-start | bytes 393224 | tf_op jit(solution)/shard_map/ppermute | solution.py:50
  11.5 13.4 %copy-start.2 = (bf16[256,256]{1,0:T(8,128)(2,1)}, bf16[256,256]{1,0:T(8,128)(2,1)S(1)}, u32[]{:S(2)}) copy-start(bf16[256,256]{1,0:T(8,128)(2,1)S(1)} %collective-permute-done.10.refs_10_.refs_5_) | copy-start | bytes 393220
  11.5 9.2 %collective-permute-start.2 = (bf16[256,256]{1,0:T(8,128)(2,1)S(1)}, bf16[256,256]{1,0:T(8,128)(2,1)S(1)}, u32[]{:S(2)}, u32[]{:S(2)}) collective-permute-start(bf16[256,256]{1,0:T(8,128)(2,1)S(1)} %join.1.refs_0_.refs_2_.refs_1_), channel_id=1, source_target_pairs={{0,12},{1,49},{4,0},{5,53},{8,4},{9,57},{12,8},{13,61},{16,28},{17... | collective-permute-start | bytes 393224 | tf_op jit(solution)/shard_map/ppermute | solution.py:50
  11.6 13.4 %copy-start.4 = (bf16[256,256]{1,0:T(8,128)(2,1)}, bf16[256,256]{1,0:T(8,128)(2,1)S(1)}, u32[]{:S(2)}) copy-start(bf16[256,256]{1,0:T(8,128)(2,1)S(1)} %collective-permute-done.9.refs_9_.refs_4_) | copy-start | bytes 393220
  11.6 9.2 %collective-permute-start.1 = (bf16[256,256]{1,0:T(8,128)(2,1)S(1)}, bf16[256,256]{1,0:T(8,128)(2,1)S(1)}, u32[]{:S(2)}, u32[]{:S(2)}) collective-permute-start(bf16[256,256]{1,0:T(8,128)(2,1)S(1)} %join.1.refs_0_.refs_2_.refs_1_), channel_id=1, source_target_pairs={{0,4},{1,17},{4,8},{5,21},{8,12},{9,25},{12,0},{13,29},{16,20},{17... | collective-permute-start | bytes 393224 | tf_op jit(solution)/shard_map/ppermute | solution.py:50
  14.2 6.6 %collective-permute-start.7 = (bf16[256,256]{1,0:T(8,128)(2,1)S(1)}, bf16[256,256]{1,0:T(8,128)(2,1)S(1)}, u32[]{:S(2)}, u32[]{:S(2)}) collective-permute-start(bf16[256,256]{1,0:T(8,128)(2,1)S(1)} %collective-permute-done.4.refs_4_), channel_id=1, source_target_pairs={{0,8},{1,33},{4,12},{5,37},{8,0},{9,41},{12,4},{13,45},{16,24},{17... | collective-permute-start | bytes 393224 | tf_op jit(solution)/shard_map/ppermute | solution.py:50
  14.3 10.6 %copy-start.6 = (bf16[256,256]{1,0:T(8,128)(2,1)}, bf16[256,256]{1,0:T(8,128)(2,1)S(1)}, u32[]{:S(2)}) copy-start(bf16[256,256]{1,0:T(8,128)(2,1)S(1)} %collective-permute-done.8.refs_8_.refs_3_) | copy-start | bytes 393220
  14.3 8.2 %collective-permute-start.6 = (bf16[256,256]{1,0:T(8,128)(2,1)S(1)}, bf16[256,256]{1,0:T(8,128)(2,1)S(1)}, u32[]{:S(2)}, u32[]{:S(2)}) collective-permute-start(bf16[256,256]{1,0:T(8,128)(2,1)S(1)} %collective-permute-done.4.refs_4_), channel_id=1, source_target_pairs={{0,12},{1,49},{4,0},{5,53},{8,4},{9,57},{12,8},{13,61},{16,28},{17... | collective-permute-start | bytes 393224 | tf_op jit(solution)/shard_map/ppermute | solution.py:50
  15.3 7.2 %collective-permute-start.5 = (bf16[256,256]{1,0:T(8,128)(2,1)S(1)}, bf16[256,256]{1,0:T(8,128)(2,1)S(1)}, u32[]{:S(2)}, u32[]{:S(2)}) collective-permute-start(bf16[256,256]{1,0:T(8,128)(2,1)S(1)} %collective-permute-done.4.refs_4_), channel_id=1, source_target_pairs={{0,4},{1,17},{4,8},{5,21},{8,12},{9,25},{12,0},{13,29},{16,20},{17... | collective-permute-start | bytes 393224 | tf_op jit(solution)/shard_map/ppermute | solution.py:50
  25.0 18.2 %collective-permute-start.11 = (bf16[1280,256]{1,0:T(8,128)(2,1)}, bf16[1280,256]{1,0:T(8,128)(2,1)S(1)}, u32[]{:S(2)}, u32[]{:S(2)}) collective-permute-start(bf16[1280,256]{1,0:T(8,128)(2,1)} %get-tuple-element.92), channel_id=1, source_target_pairs={{0,16},{1,5},{4,20},{5,9},{8,24},{9,13},{12,28},{13,1},{16,32},{17... | collective-permute-start | bytes 1966088 | tf_op jit(solution)/shard_map/ppermute | solution.py:50
  25.1 18.2 %collective-permute-start.12 = (bf16[1280,256]{1,0:T(8,128)(2,1)}, bf16[1280,256]{1,0:T(8,128)(2,1)S(1)}, u32[]{:S(2)}, u32[]{:S(2)}) collective-permute-start(bf16[1280,256]{1,0:T(8,128)(2,1)} %get-tuple-element.93), channel_id=1, source_target_pairs={{0,48},{1,13},{4,52},{5,1},{8,56},{9,5},{12,60},{13,9},{16,0},{17,... | collective-permute-start | bytes 1966088 | tf_op jit(solution)/shard_map/ppermute | solution.py:50
  27.7 27.6 %collective-permute-start.13 = (bf16[1280,256]{1,0:T(8,128)(2,1)}, bf16[1280,256]{1,0:T(8,128)(2,1)S(1)}, u32[]{:S(2)}, u32[]{:S(2)}) collective-permute-start(bf16[1280,256]{1,0:T(8,128)(2,1)} %get-tuple-element.94), channel_id=1, source_target_pairs={{0,32},{1,9},{4,36},{5,13},{8,40},{9,1},{12,44},{13,5},{16,48},{17... | collective-permute-start | bytes 1966088 | tf_op jit(solution)/shard_map/ppermute | solution.py:50
  28.3 1.1 %copy-start.1 = (bf16[256,896]{1,0:T(8,128)(2,1)S(1)}, bf16[256,896]{1,0:T(8,128)(2,1)}, u32[]{:S(2)}) copy-start(bf16[256,896]{1,0:T(8,128)(2,1)} %refs_0_.1) | copy-start | bytes 1376260
  29.4 7.0 %copy-start.3 = (bf16[256,256]{1,0:T(8,128)(2,1)S(1)}, bf16[256,256]{1,0:T(8,128)(2,1)}, u32[]{:S(2)}) copy-start(bf16[256,256]{1,0:T(8,128)(2,1)} %copy-done.2) | copy-start | bytes 393220
  29.4 7.0 %copy-start.5 = (bf16[256,256]{1,0:T(8,128)(2,1)S(1)}, bf16[256,256]{1,0:T(8,128)(2,1)}, u32[]{:S(2)}) copy-start(bf16[256,256]{1,0:T(8,128)(2,1)} %copy-done.4) | copy-start | bytes 393220
  29.4 7.0 %copy-start.7 = (bf16[256,256]{1,0:T(8,128)(2,1)S(1)}, bf16[256,256]{1,0:T(8,128)(2,1)}, u32[]{:S(2)}) copy-start(bf16[256,256]{1,0:T(8,128)(2,1)} %copy-done.6) | copy-start | bytes 393220
  29.4 7.0 %copy-start.8 = (bf16[2304,256]{1,0:T(8,128)(2,1)S(1)}, bf16[2304,256]{1,0:T(8,128)(2,1)}, u32[]{:S(2)}) copy-start(bf16[2304,256]{1,0:T(8,128)(2,1)} %get-tuple-element.156.refs_6_) | copy-start | bytes 3538948
  29.5 7.0 %copy-start.10 = (bf16[256,256]{1,0:T(8,128)(2,1)S(1)}, bf16[256,256]{1,0:T(8,128)(2,1)}, u32[]{:S(2)}) copy-start(bf16[256,256]{1,0:T(8,128)(2,1)} %copy-done.9) | copy-start | bytes 393220
  62.0 13.1 %collective-permute-start.14 = (bf16[256,512]{1,0:T(8,128)(2,1)}, bf16[256,512]{1,0:T(8,128)(2,1)S(1)}, u32[]{:S(2)}, u32[]{:S(2)}) collective-permute-start(bf16[256,512]{1,0:T(8,128)(2,1)} %get-tuple-element.100.refs_0_), channel_id=1, source_target_pairs={{0,1},{1,0},{2,3},{3,2},{4,5},{5,4},{6,7},{7,6},{8,9},{9,8},{10,11... | collective-permute-start | bytes 786440 | tf_op jit(solution)/shard_map/ppermute | solution.py:62
  73.3 1.7 %collective-permute-start.15 = (bf16[256,384]{1,0:T(8,128)(2,1)S(1)}, bf16[256,384]{1,0:T(8,128)(2,1)S(1)}, u32[]{:S(2)}, u32[]{:S(2)}) collective-permute-start(bf16[256,384]{1,0:T(8,128)(2,1)S(1)} %last.3.refs_1_), channel_id=1, source_target_pairs={{0,1},{1,0},{2,3},{3,2},{4,5},{5,4},{6,7},{7,6},{8,9},{9,8},{10,11... | collective-permute-start | bytes 589832 | tf_op jit(solution)/shard_map/ppermute | solution.py:62
  73.4 12.0 %collective-permute-start.16 = (bf16[256,512]{1,0:T(8,128)(2,1)}, bf16[256,512]{1,0:T(8,128)(2,1)S(1)}, u32[]{:S(2)}, u32[]{:S(2)}) collective-permute-start(bf16[256,512]{1,0:T(8,128)(2,1)} %get-tuple-element.100.refs_0_), channel_id=1, source_target_pairs={{0,2},{2,0},{1,3},{3,1},{4,6},{6,4},{5,7},{7,5},{8,10},{10,8},{9,1... | collective-permute-start | bytes 786440 | tf_op jit(solution)/shard_map/ppermute | solution.py:62
  74.2 11.2 %collective-permute-start.17 = (bf16[256,384]{1,0:T(8,128)(2,1)S(1)}, bf16[256,384]{1,0:T(8,128)(2,1)S(1)}, u32[]{:S(2)}, u32[]{:S(2)}) collective-permute-start(bf16[256,384]{1,0:T(8,128)(2,1)S(1)} %last.3.refs_1_), channel_id=1, source_target_pairs={{0,2},{2,0},{1,3},{3,1},{4,6},{6,4},{5,7},{7,5},{8,10},{10,8},{9,1... | collective-permute-start | bytes 589832 | tf_op jit(solution)/shard_map/ppermute | solution.py:62
  75.1 2.8 %copy-start = (bf16[3584,896]{1,0:T(8,128)(2,1)S(1)}, bf16[3584,896]{1,0:T(8,128)(2,1)}, u32[]{:S(2)}) copy-start(bf16[3584,896]{1,0:T(8,128)(2,1)} %weight.1) | copy-start | bytes 19267588
  85.4 2.7 %collective-permute-start.18 = (bf16[256,512]{1,0:T(8,128)(2,1)S(1)}, bf16[256,512]{1,0:T(8,128)(2,1)S(1)}, u32[]{:S(2)}, u32[]{:S(2)}) collective-permute-start(bf16[256,512]{1,0:T(8,128)(2,1)S(1)} %collective-permute-done.16.refs_0_), channel_id=1, source_target_pairs={{0,1},{1,0},{2,3},{3,2},{4,5},{5,4},{6,7},{7,6},{8,9},{9,8},{10,11... | collective-permute-start | bytes 786440 | tf_op jit(solution)/shard_map/ppermute | solution.py:62
  86.7 1.4 %collective-permute-start.19 = (bf16[256,384]{1,0:T(8,128)(2,1)S(1)}, bf16[256,384]{1,0:T(8,128)(2,1)S(1)}, u32[]{:S(2)}, u32[]{:S(2)}) collective-permute-start(bf16[256,384]{1,0:T(8,128)(2,1)S(1)} %collective-permute-done.17.refs_2_), channel_id=1, source_target_pairs={{0,1},{1,0},{2,3},{3,2},{4,5},{5,4},{6,7},{7,6},{8,9},{9,8},{10,11... | collective-permute-start | bytes 589832 | tf_op jit(solution)/shard_map/ppermute | solution.py:62

commit v4 on v3

--- a/solution.py
+++ b/solution.py
@@ -23,7 +23,7 @@
 SMALL = 256
 NEAR_BLOCKS = 3
 FAR_BLOCKS = 9
-CHUNKS = ((0, 4), (4, 7))
+CHUNKS = ((0, 5), (5, 7))
 TILE = 896
 FLAG = HEADS * TOK
 SCALE = 1.4426950408889634 / HD**0.5

time: 90.9 us -> 87.3 us (0.960)
  waiting for transfers between devices: 13.7 us -> 10.4 us
    ppermute x7, waiting for transfers between devices: 6.15 us -> 2.79 us  [swap(): return lax.ppermute(block, axis, [(0, 1), (1, 0)])]
  transfers between devices with their start and end apart: 19 -> 19, of which waited for: 5 -> 6; matrix products, arithmetic and copies ran while one was open for 2% -> 2% of each run, Pallas kernels for 30% -> 30%
where the time goes in v4:
time: 87.3 us; the launch traced here: 87 us
  Pallas kernels  40 us (46%)
  starting transfers between devices  31.1 us (36%)
  waiting for transfers between devices  10.4 us (12%)
  local copies, waits for them, and re-layouts  4.72 us (5%)
    ppermute x9, starting transfers between devices, move(): return lax.ppermute(block, ('y', 'x', 'c'), turn(by_first, by_second))  14.3 us
    ppermute x7, starting transfers between devices, swap(): return lax.ppermute(block, axis, [(0, 1), (1, 0)])  13.9 us
    pallas_call x1, Pallas kernels, attend_middle(): pl.pallas_call(kernel, out_shape=STATE, in_specs=[SMEM] + [VMEM] * 5 + [H...  12.1 us
    pallas_call x2, Pallas kernels, attend_last(): pl.pallas_call(functools.partial(last_kernel, low, high), out_shape=shape...  11.2 us
    ppermute x9, waiting for transfers between devices, move(): return lax.ppermute(block, ('y', 'x', 'c'), turn(by_first, by_second))  7.45 us
    pallas_call x1, Pallas kernels, attend_own(): pl.pallas_call(own_kernel, out_shape=[rows] + STATE, in_specs=[SMEM, VMEM...  6.92 us
    pallas_call x2, Pallas kernels, project(): pl.pallas_call(functools.partial(kernel, where), out_shape=out_shape, in_...  5.38 us
    ppermute x3, starting transfers between devices, ring(): return lax.ppermute(block, ('zh', 'y', 'x'), pairs)  2.9 us
  transfers between devices with their start and end apart: 19, of which 6 were waited for; matrix products, arithmetic and copies ran while one was open for 2% of the time, Pallas kernels for 30%

profile of v4, /device:TPU:25, one launch (start us, length us, event | category | flops | bytes accessed | tf_op | source)
XLA Modules:
  0.0 87.0 jit_solution(4527322895090191591)
XLA Ops:
  0.0 0.9 %join.1.refs_0_.refs_2_.refs_1_ = bf16[256,256]{1,0:T(8,128)(2,1)S(1)} custom-call(bf16[256,128]{1,0:T(8,128)(2,1)} %keys.1, bf16[256,128]{1,0:T(8,128)(2,1)} %values.1), custom_call_target="tpu_custom_call" | custom-call | tf_op jit(solution)/shard_map/join/pallas_call | solution.py:124
  0.9 0.0 copy-start.9
  0.9 2.5 %collective-permute-start.10 = (bf16[256,256]{1,0:T(8,128)(2,1)S(1)}, bf16[256,256]{1,0:T(8,128)(2,1)S(1)}, u32[]{:S(2)}, u32[]{:S(2)}) collective-permute-start(bf16[256,256]{1,0:T(8,128)(2,1)S(1)} %join.1.refs_0_.refs_2_.refs_1_), channel_id=1, source_target_pairs={{0,12},{64,116},{4,16},{68,120},{8,20},{72,124},{12,24},{76,64},{1... | collective-permute-start | bytes 393224 | tf_op jit(solution)/shard_map/ppermute | solution.py:58
  3.5 0.3 collective-permute-start.9
  3.8 4.5 %collective-permute-start.4 = (bf16[256,256]{1,0:T(8,128)(2,1)S(1)}, bf16[256,256]{1,0:T(8,128)(2,1)S(1)}, u32[]{:S(2)}, u32[]{:S(2)}) collective-permute-start(bf16[256,256]{1,0:T(8,128)(2,1)S(1)} %join.1.refs_0_.refs_2_.refs_1_), channel_id=1, source_target_pairs={{0,64},{64,0},{1,65},{65,1},{2,66},{66,2},{3,67},{67,3},{4,68},{68... | collective-permute-start | bytes 393224 | tf_op jit(solution)/shard_map/ppermute | solution.py:62
  8.3 0.0 collective-permute-start.8
  8.3 3.2 %collective-permute-start.3 = (bf16[256,256]{1,0:T(8,128)(2,1)S(1)}, bf16[256,256]{1,0:T(8,128)(2,1)S(1)}, u32[]{:S(2)}, u32[]{:S(2)}) collective-permute-start(bf16[256,256]{1,0:T(8,128)(2,1)S(1)} %join.1.refs_0_.refs_2_.refs_1_), channel_id=1, source_target_pairs={{0,8},{1,33},{4,12},{5,37},{8,0},{9,41},{12,4},{13,45},{16,24},{17... | collective-permute-start | bytes 393224 | tf_op jit(solution)/shard_map/ppermute | solution.py:50
  11.5 0.0 collective-permute-done.10.refs_10_.refs_5_
  11.5 0.0 collective-permute-start.2
  11.5 0.0 collective-permute-done.9.refs_9_.refs_4_
  11.6 0.0 copy-start.4
  11.6 2.7 %collective-permute-start.1 = (bf16[256,256]{1,0:T(8,128)(2,1)S(1)}, bf16[256,256]{1,0:T(8,128)(2,1)S(1)}, u32[]{:S(2)}, u32[]{:S(2)}) collective-permute-start(bf16[256,256]{1,0:T(8,128)(2,1)S(1)} %join.1.refs_0_.refs_2_.refs_1_), channel_id=1, source_target_pairs={{0,4},{1,17},{4,8},{5,21},{8,12},{9,25},{12,0},{13,29},{16,20},{17... | collective-permute-start | bytes 393224 | tf_op jit(solution)/shard_map/ppermute | solution.py:50
  14.2 0.0 collective-permute-done.4.refs_4_
  14.2 0.0 collective-permute-start.7
  14.2 0.1 collective-permute-done.8.refs_8_.refs_3_
  14.3 1.0 %collective-permute-start.6 = (bf16[256,256]{1,0:T(8,128)(2,1)S(1)}, bf16[256,256]{1,0:T(8,128)(2,1)S(1)}, u32[]{:S(2)}, u32[]{:S(2)}) collective-permute-start(bf16[256,256]{1,0:T(8,128)(2,1)S(1)} %collective-permute-done.4.refs_4_), channel_id=1, source_target_pairs={{0,12},{1,49},{4,0},{5,53},{8,4},{9,57},{12,8},{13,61},{16,28},{17... | collective-permute-start | bytes 393224 | tf_op jit(solution)/shard_map/ppermute | solution.py:50
  15.3 0.0 collective-permute-done.3.refs_3_.refs_4_
  15.3 4.7 %collective-permute-start.5 = (bf16[256,256]{1,0:T(8,128)(2,1)S(1)}, bf16[256,256]{1,0:T(8,128)(2,1)S(1)}, u32[]{:S(2)}, u32[]{:S(2)}) collective-permute-start(bf16[256,256]{1,0:T(8,128)(2,1)S(1)} %collective-permute-done.4.refs_4_), channel_id=1, source_target_pairs={{0,4},{1,17},{4,8},{5,21},{8,12},{9,25},{12,0},{13,29},{16,20},{17... | collective-permute-start | bytes 393224 | tf_op jit(solution)/shard_map/ppermute | solution.py:50
  20.0 0.7 concatenate.3.table.refs_0_
  20.8 0.0 collective-permute-done.2.refs_2_.refs_3_
  20.8 0.0 collective-permute-done.1.refs_1_.refs_2_
  20.8 0.0 collective-permute-done.7.refs_7_
  20.8 1.8 %collective-permute-done.6.refs_6_ = bf16[256,256]{1,0:T(8,128)(2,1)S(1)} collective-permute-done((bf16[256,256]{1,0:T(8,128)(2,1)S(1)}, bf16[256,256]{1,0:T(8,128)(2,1)S(1)}, u32[]{:S(2)}, u32[]{:S(2)}) %collective-permute-start.6) | collective-permute-done | bytes 131104 | tf_op jit(solution)/shard_map/ppermute | solution.py:50
  22.6 0.0 collective-permute-done.5.refs_5_
  22.6 2.4 %pack.1 = (bf16[1280,256]{1,0:T(8,128)(2,1)S(1)}, bf16[1280,256]{1,0:T(8,128)(2,1)}, bf16[1280,256]{1,0:T(8,128)(2,1)}, bf16[1280,256]{1,0:T(8,128)(2,1)}, s32[1]{0:T(128)}) custom-call(s32[20]{0:T(128)S(1)} %concatenate.3.table.refs_0_, bf16[256,256]{1,0:T(8,128)(2,1)S(1)} %join.1.refs_0_.refs_2_.refs_1_, ...), custom_call_target="tpu_custom_call" | custom-call | tf_op jit(solution)/shard_map/pack/pallas_call | solution.py:182
  24.9 0.0 copy-done.2
  25.0 0.0 copy-done.4
  25.0 0.0 copy-done.6
  25.0 0.1 collective-permute-start.11
  25.1 0.0 copy-done.9
  25.1 2.7 %collective-permute-start.12 = (bf16[1280,256]{1,0:T(8,128)(2,1)}, bf16[1280,256]{1,0:T(8,128)(2,1)S(1)}, u32[]{:S(2)}, u32[]{:S(2)}) collective-permute-start(bf16[1280,256]{1,0:T(8,128)(2,1)} %get-tuple-element.93), channel_id=1, source_target_pairs={{0,48},{1,13},{4,52},{5,1},{8,56},{9,5},{12,60},{13,9},{16,0},{17,... | collective-permute-start | bytes 1966088 | tf_op jit(solution)/shard_map/ppermute | solution.py:50
  27.7 0.0 collective-permute-start.13
  28.3 0.0 copy-start.1
  28.3 1.1 %conditional.1 = (bf16[2304,256]{1,0:T(8,128)(2,1)}) conditional(s32[]{:T(128)} %bitcast.8, () %tuple.26, bf16[256,256]{1,0:T(8,128)(2,1)} %copy-done.9), branch_computations={%region_0.0_spmd, %region_1.0_spmd} | conditional | flops 8 | bytes 2490649 | solution.py:596
  28.3 1.1 %broadcast_in_dim.4 = bf16[2304,256]{1,0:T(8,128)(2,1)} broadcast(bf16[]{:T(256)} %constant.50.clone), dimensions={} | broadcast | bytes 1179650 | tf_op jit(solution)/shard_map/broadcast_in_dim | solution.py:585
  29.4 0.0 copy-done.1
  29.4 0.0 copy-start.8
  29.4 0.0 copy-start.10
  29.5 6.9 %own.1 = (bf16[1792,128]{1,0:T(8,128)(2,1)S(1)}, f32[1800,128]{1,0:T(8,128)S(1)}, f32[1792,256]{1,0:T(8,128)S(1)}) custom-call(s32[20]{0:T(128)S(1)} %concatenate.3.table.refs_0_, bf16[256,896]{1,0:T(8,128)(2,1)S(1)} %copy-done.1, bf16[1280,256]{1,0:T(8,128)(2,1)S(1)} %get-tuple-element.90.own), custom_call_target="tpu_custom_call" | custom-call | flops 1409286144 | bytes 917504 | tf_op jit(solution)/shard_map/own/pallas_call | solution.py:468
  36.4 0.0 copy-done.3
  36.4 0.0 copy-done.5
  36.4 1.1 %small.1.refs_6_ = bf16[256,896]{1,0:T(8,128)(2,1)S(1)} custom-call(s32[20]{0:T(128)S(1)} %concatenate.3.table.refs_0_, s32[1]{0:T(128)} %get-tuple-element.95.refs_0_, bf16[256,896]{1,0:T(8,128)(2,1)S(1)} %copy-done.1, bf16[256,256]{1,0:T(8,128)(2,1)S(1)} %copy-done.10, bf16[256,256]{1,0:T(8,128)(2,1)S(1)} %copy-done.7, bf16[256,256]{1,0:T(8,128)(2,1)S(1)} %copy-done.5, ...), custom_call_target="tpu_custom_call" | custom-call | flops 352321536 | bytes 917504 | tf_op jit(solution)/shard_map/small/pallas_call | solution.py:517
  37.6 5.7 %collective-permute-done.11.refs_2_.b1 = bf16[1280,256]{1,0:T(8,128)(2,1)S(1)} collective-permute-done((bf16[1280,256]{1,0:T(8,128)(2,1)}, bf16[1280,256]{1,0:T(8,128)(2,1)S(1)}, u32[]{:S(2)}, u32[]{:S(2)}) %collective-permute-start.11) | collective-permute-done | bytes 655392 | tf_op jit(solution)/shard_map/ppermute | solution.py:50
  43.2 0.0 collective-permute-done.12.refs_3_.b2
  43.2 12.1 %middle.1 = (f32[1800,128]{1,0:T(8,128)S(1)}, f32[1792,256]{1,0:T(8,128)S(1)}) custom-call(s32[20]{0:T(128)S(1)} %concatenate.3.table.refs_0_, bf16[1792,128]{1,0:T(8,128)(2,1)S(1)} %get-tuple-element.91.refs_7_.refs_1_.rows_in, bf16[1280,256]{1,0:T(8,128)(2,1)S(1)} %collective-permute-done.11.refs_2_.b1, ...), custom_call_target="tpu_custom_call", output_to_operand_aliasing={{0}: (4, {}), {1}: (5, {})} | custom-call | flops 2818572288 | bytes 917504 | tf_op jit(solution)/shard_map/middle/pallas_call | solution.py:484
  55.4 0.0 collective-permute-done.13.b3
  55.4 7.7 %last.2 = (bf16[256,640]{1,0:T(8,128)(2,1)}, bf16[256,256]{1,0:T(8,128)(2,1)S(1)}) custom-call(s32[20]{0:T(128)S(1)} %concatenate.3.table.refs_0_, bf16[1792,128]{1,0:T(8,128)(2,1)S(1)} %get-tuple-element.91.refs_7_.refs_1_.rows_in, bf16[1280,256]{1,0:T(8,128)(2,1)S(1)} %get-tuple-element.90.own, bf16[1280,256]{1,0:T(8,128)(2,1)S(1)} %collective-permute-done.11.refs_2_.b1, ...), custom_call_target="tpu_custom_call" | custom-call | flops 1258291200 | bytes 655360 | tf_op jit(solution)/shard_map/last/pallas_call | solution.py:504
  63.1 6.7 %collective-permute-start.14 = (bf16[256,640]{1,0:T(8,128)(2,1)}, bf16[256,640]{1,0:T(8,128)(2,1)S(1)}, u32[]{:S(2)}, u32[]{:S(2)}) collective-permute-start(bf16[256,640]{1,0:T(8,128)(2,1)} %get-tuple-element.100.refs_0_), channel_id=1, source_target_pairs={{0,1},{1,0},{2,3},{3,2},{4,5},{5,4},{6,7},{7,6},{8,9},{9,8},{10,11... | collective-permute-start | bytes 983048 | tf_op jit(solution)/shard_map/ppermute | solution.py:62
  69.9 0.7 collective-permute-start.16
  70.6 3.4 %last.3.refs_1_ = bf16[256,256]{1,0:T(8,128)(2,1)S(1)} custom-call(s32[20]{0:T(128)S(1)} %concatenate.3.table.refs_0_, bf16[1792,128]{1,0:T(8,128)(2,1)S(1)} %get-tuple-element.91.refs_7_.refs_1_.rows_in, bf16[1280,256]{1,0:T(8,128)(2,1)S(1)} %get-tuple-element.90.own, bf16[1280,256]{1,0:T(8,128)(2,1)S(1)} %collective-permute-done.11.refs_2_.b1, ...), custom_call_target="tpu_custom_call" | custom-call | flops 503316480 | bytes 262144 | tf_op jit(solution)/shard_map/last/pallas_call | solution.py:504
  74.0 0.4 collective-permute-start.15
  74.4 0.8 collective-permute-start.17
  75.1 0.1 pad_add_fusion.groups
  75.2 0.2 collective-permute-done.15.refs_3_
  75.5 0.0 collective-permute-done.14.refs_2_
  75.5 2.8 %copy-done = bf16[3584,896]{1,0:T(8,128)(2,1)S(1)} copy-done((bf16[3584,896]{1,0:T(8,128)(2,1)S(1)}, bf16[3584,896]{1,0:T(8,128)(2,1)}, u32[]{:S(2)}) %copy-start) | copy-done | bytes 6422552
  78.3 2.8 %project.2 = (f32[256,896]{1,0:T(8,128)S(1)}, bf16[3584,896]{1,0:T(8,128)(2,1)S(1)}) custom-call(s32[4]{0:T(128)S(1)} %pad_add_fusion.groups, bf16[3584,896]{1,0:T(8,128)(2,1)S(1)} %copy-done, bf16[256,640]{1,0:T(8,128)(2,1)} %get-tuple-element.100.refs_0_, bf16[256,256]{1,0:T(8,128)(2,1)S(1)} %last.3.refs_1_, ...), custom_call_target="tpu_custom_call" | custom-call | flops 822083584 | bytes 3211264 | tf_op jit(solution)/shard_map/project/pallas_call | solution.py:561
  81.1 1.1 %collective-permute-done.17.refs_2_ = bf16[256,256]{1,0:T(8,128)(2,1)S(1)} collective-permute-done((bf16[256,256]{1,0:T(8,128)(2,1)S(1)}, bf16[256,256]{1,0:T(8,128)(2,1)S(1)}, u32[]{:S(2)}, u32[]{:S(2)}) %collective-permute-start.17) | collective-permute-done | bytes 131104 | tf_op jit(solution)/shard_map/ppermute | solution.py:62
  82.2 0.0 collective-permute-done.16.refs_0_
  82.2 0.8 collective-permute-start.18
  83.0 0.0 collective-permute-start.19
  83.0 1.4 %collective-permute-done.19.refs_3_ = bf16[256,256]{1,0:T(8,128)(2,1)S(1)} collective-permute-done((bf16[256,256]{1,0:T(8,128)(2,1)S(1)}, bf16[256,256]{1,0:T(8,128)(2,1)S(1)}, u32[]{:S(2)}, u32[]{:S(2)}) %collective-permute-start.19) | collective-permute-done | bytes 131104 | tf_op jit(solution)/shard_map/ppermute | solution.py:62
  84.5 0.0 collective-permute-done.18.refs_1_
  84.5 2.5 %project.3 = bf16[256,896]{1,0:T(8,128)(2,1)} custom-call(s32[4]{0:T(128)S(1)} %pad_add_fusion.groups, bf16[3584,896]{1,0:T(8,128)(2,1)S(1)} %get-tuple-element.102.weight, bf16[256,640]{1,0:T(8,128)(2,1)S(1)} %collective-permute-done.16.refs_0_, bf16[256,640]{1,0:T(8,128)(2,1)S(1)} %collective-permute-done.18.refs_1_, ...), custom_call_target="tpu_custom_call" | custom-call | flops 822083584 | bytes 3211264 | tf_op jit(solution)/shard_map/project/pallas_call | solution.py:561
  (9 shorter events, 0.0 us)
Async XLA Ops:
  0.9 24.2 %copy-start.9 = (bf16[256,256]{1,0:T(8,128)(2,1)}, bf16[256,256]{1,0:T(8,128)(2,1)S(1)}, u32[]{:S(2)}) copy-start(bf16[256,256]{1,0:T(8,128)(2,1)S(1)} %join.1.refs_0_.refs_2_.refs_1_) | copy-start | bytes 393220
  0.9 10.6 %collective-permute-start.10 = (bf16[256,256]{1,0:T(8,128)(2,1)S(1)}, bf16[256,256]{1,0:T(8,128)(2,1)S(1)}, u32[]{:S(2)}, u32[]{:S(2)}) collective-permute-start(bf16[256,256]{1,0:T(8,128)(2,1)S(1)} %join.1.refs_0_.refs_2_.refs_1_), channel_id=1, source_target_pairs={{0,12},{64,116},{4,16},{68,120},{8,20},{72,124},{12,24},{76,64},{1... | collective-permute-start | bytes 393224 | tf_op jit(solution)/shard_map/ppermute | solution.py:58
  3.5 8.1 %collective-permute-start.9 = (bf16[256,256]{1,0:T(8,128)(2,1)S(1)}, bf16[256,256]{1,0:T(8,128)(2,1)S(1)}, u32[]{:S(2)}, u32[]{:S(2)}) collective-permute-start(bf16[256,256]{1,0:T(8,128)(2,1)S(1)} %join.1.refs_0_.refs_2_.refs_1_), channel_id=1, source_target_pairs={{0,8},{64,120},{4,12},{68,124},{8,16},{72,64},{12,20},{76,68},{16,... | collective-permute-start | bytes 393224 | tf_op jit(solution)/shard_map/ppermute | solution.py:58
  3.8 10.4 %collective-permute-start.4 = (bf16[256,256]{1,0:T(8,128)(2,1)S(1)}, bf16[256,256]{1,0:T(8,128)(2,1)S(1)}, u32[]{:S(2)}, u32[]{:S(2)}) collective-permute-start(bf16[256,256]{1,0:T(8,128)(2,1)S(1)} %join.1.refs_0_.refs_2_.refs_1_), channel_id=1, source_target_pairs={{0,64},{64,0},{1,65},{65,1},{2,66},{66,2},{3,67},{67,3},{4,68},{68... | collective-permute-start | bytes 393224 | tf_op jit(solution)/shard_map/ppermute | solution.py:62
  8.3 6.0 %collective-permute-start.8 = (bf16[256,256]{1,0:T(8,128)(2,1)S(1)}, bf16[256,256]{1,0:T(8,128)(2,1)S(1)}, u32[]{:S(2)}, u32[]{:S(2)}) collective-permute-start(bf16[256,256]{1,0:T(8,128)(2,1)S(1)} %join.1.refs_0_.refs_2_.refs_1_), channel_id=1, source_target_pairs={{0,4},{64,124},{4,8},{68,64},{8,12},{72,68},{12,16},{76,72},{16,20... | collective-permute-start | bytes 393224 | tf_op jit(solution)/shard_map/ppermute | solution.py:58
  8.3 7.0 %collective-permute-start.3 = (bf16[256,256]{1,0:T(8,128)(2,1)S(1)}, bf16[256,256]{1,0:T(8,128)(2,1)S(1)}, u32[]{:S(2)}, u32[]{:S(2)}) collective-permute-start(bf16[256,256]{1,0:T(8,128)(2,1)S(1)} %join.1.refs_0_.refs_2_.refs_1_), channel_id=1, source_target_pairs={{0,8},{1,33},{4,12},{5,37},{8,0},{9,41},{12,4},{13,45},{16,24},{17... | collective-permute-start | bytes 393224 | tf_op jit(solution)/shard_map/ppermute | solution.py:50
  11.5 13.4 %copy-start.2 = (bf16[256,256]{1,0:T(8,128)(2,1)}, bf16[256,256]{1,0:T(8,128)(2,1)S(1)}, u32[]{:S(2)}) copy-start(bf16[256,256]{1,0:T(8,128)(2,1)S(1)} %collective-permute-done.10.refs_10_.refs_5_) | copy-start | bytes 393220
  11.5 9.2 %collective-permute-start.2 = (bf16[256,256]{1,0:T(8,128)(2,1)S(1)}, bf16[256,256]{1,0:T(8,128)(2,1)S(1)}, u32[]{:S(2)}, u32[]{:S(2)}) collective-permute-start(bf16[256,256]{1,0:T(8,128)(2,1)S(1)} %join.1.refs_0_.refs_2_.refs_1_), channel_id=1, source_target_pairs={{0,12},{1,49},{4,0},{5,53},{8,4},{9,57},{12,8},{13,61},{16,28},{17... | collective-permute-start | bytes 393224 | tf_op jit(solution)/shard_map/ppermute | solution.py:50
  11.6 13.4 %copy-start.4 = (bf16[256,256]{1,0:T(8,128)(2,1)}, bf16[256,256]{1,0:T(8,128)(2,1)S(1)}, u32[]{:S(2)}) copy-start(bf16[256,256]{1,0:T(8,128)(2,1)S(1)} %collective-permute-done.9.refs_9_.refs_4_) | copy-start | bytes 393220
  11.6 9.2 %collective-permute-start.1 = (bf16[256,256]{1,0:T(8,128)(2,1)S(1)}, bf16[256,256]{1,0:T(8,128)(2,1)S(1)}, u32[]{:S(2)}, u32[]{:S(2)}) collective-permute-start(bf16[256,256]{1,0:T(8,128)(2,1)S(1)} %join.1.refs_0_.refs_2_.refs_1_), channel_id=1, source_target_pairs={{0,4},{1,17},{4,8},{5,21},{8,12},{9,25},{12,0},{13,29},{16,20},{17... | collective-permute-start | bytes 393224 | tf_op jit(solution)/shard_map/ppermute | solution.py:50
  14.2 6.6 %collective-permute-start.7 = (bf16[256,256]{1,0:T(8,128)(2,1)S(1)}, bf16[256,256]{1,0:T(8,128)(2,1)S(1)}, u32[]{:S(2)}, u32[]{:S(2)}) collective-permute-start(bf16[256,256]{1,0:T(8,128)(2,1)S(1)} %collective-permute-done.4.refs_4_), channel_id=1, source_target_pairs={{0,8},{1,33},{4,12},{5,37},{8,0},{9,41},{12,4},{13,45},{16,24},{17... | collective-permute-start | bytes 393224 | tf_op jit(solution)/shard_map/ppermute | solution.py:50
  14.3 10.6 %copy-start.6 = (bf16[256,256]{1,0:T(8,128)(2,1)}, bf16[256,256]{1,0:T(8,128)(2,1)S(1)}, u32[]{:S(2)}) copy-start(bf16[256,256]{1,0:T(8,128)(2,1)S(1)} %collective-permute-done.8.refs_8_.refs_3_) | copy-start | bytes 393220
  14.3 8.2 %collective-permute-start.6 = (bf16[256,256]{1,0:T(8,128)(2,1)S(1)}, bf16[256,256]{1,0:T(8,128)(2,1)S(1)}, u32[]{:S(2)}, u32[]{:S(2)}) collective-permute-start(bf16[256,256]{1,0:T(8,128)(2,1)S(1)} %collective-permute-done.4.refs_4_), channel_id=1, source_target_pairs={{0,12},{1,49},{4,0},{5,53},{8,4},{9,57},{12,8},{13,61},{16,28},{17... | collective-permute-start | bytes 393224 | tf_op jit(solution)/shard_map/ppermute | solution.py:50
  15.3 7.2 %collective-permute-start.5 = (bf16[256,256]{1,0:T(8,128)(2,1)S(1)}, bf16[256,256]{1,0:T(8,128)(2,1)S(1)}, u32[]{:S(2)}, u32[]{:S(2)}) collective-permute-start(bf16[256,256]{1,0:T(8,128)(2,1)S(1)} %collective-permute-done.4.refs_4_), channel_id=1, source_target_pairs={{0,4},{1,17},{4,8},{5,21},{8,12},{9,25},{12,0},{13,29},{16,20},{17... | collective-permute-start | bytes 393224 | tf_op jit(solution)/shard_map/ppermute | solution.py:50
  25.0 18.2 %collective-permute-start.11 = (bf16[1280,256]{1,0:T(8,128)(2,1)}, bf16[1280,256]{1,0:T(8,128)(2,1)S(1)}, u32[]{:S(2)}, u32[]{:S(2)}) collective-permute-start(bf16[1280,256]{1,0:T(8,128)(2,1)} %get-tuple-element.92), channel_id=1, source_target_pairs={{0,16},{1,5},{4,20},{5,9},{8,24},{9,13},{12,28},{13,1},{16,32},{17... | collective-permute-start | bytes 1966088 | tf_op jit(solution)/shard_map/ppermute | solution.py:50
  25.1 18.2 %collective-permute-start.12 = (bf16[1280,256]{1,0:T(8,128)(2,1)}, bf16[1280,256]{1,0:T(8,128)(2,1)S(1)}, u32[]{:S(2)}, u32[]{:S(2)}) collective-permute-start(bf16[1280,256]{1,0:T(8,128)(2,1)} %get-tuple-element.93), channel_id=1, source_target_pairs={{0,48},{1,13},{4,52},{5,1},{8,56},{9,5},{12,60},{13,9},{16,0},{17,... | collective-permute-start | bytes 1966088 | tf_op jit(solution)/shard_map/ppermute | solution.py:50
  27.7 27.6 %collective-permute-start.13 = (bf16[1280,256]{1,0:T(8,128)(2,1)}, bf16[1280,256]{1,0:T(8,128)(2,1)S(1)}, u32[]{:S(2)}, u32[]{:S(2)}) collective-permute-start(bf16[1280,256]{1,0:T(8,128)(2,1)} %get-tuple-element.94), channel_id=1, source_target_pairs={{0,32},{1,9},{4,36},{5,13},{8,40},{9,1},{12,44},{13,5},{16,48},{17... | collective-permute-start | bytes 1966088 | tf_op jit(solution)/shard_map/ppermute | solution.py:50
  28.3 1.1 %copy-start.1 = (bf16[256,896]{1,0:T(8,128)(2,1)S(1)}, bf16[256,896]{1,0:T(8,128)(2,1)}, u32[]{:S(2)}) copy-start(bf16[256,896]{1,0:T(8,128)(2,1)} %refs_0_.1) | copy-start | bytes 1376260
  29.4 7.0 %copy-start.3 = (bf16[256,256]{1,0:T(8,128)(2,1)S(1)}, bf16[256,256]{1,0:T(8,128)(2,1)}, u32[]{:S(2)}) copy-start(bf16[256,256]{1,0:T(8,128)(2,1)} %copy-done.2) | copy-start | bytes 393220
  29.4 7.0 %copy-start.5 = (bf16[256,256]{1,0:T(8,128)(2,1)S(1)}, bf16[256,256]{1,0:T(8,128)(2,1)}, u32[]{:S(2)}) copy-start(bf16[256,256]{1,0:T(8,128)(2,1)} %copy-done.4) | copy-start | bytes 393220
  29.4 7.0 %copy-start.7 = (bf16[256,256]{1,0:T(8,128)(2,1)S(1)}, bf16[256,256]{1,0:T(8,128)(2,1)}, u32[]{:S(2)}) copy-start(bf16[256,256]{1,0:T(8,128)(2,1)} %copy-done.6) | copy-start | bytes 393220
  29.4 7.0 %copy-start.8 = (bf16[2304,256]{1,0:T(8,128)(2,1)S(1)}, bf16[2304,256]{1,0:T(8,128)(2,1)}, u32[]{:S(2)}) copy-start(bf16[2304,256]{1,0:T(8,128)(2,1)} %get-tuple-element.156.refs_6_) | copy-start | bytes 3538948
  29.4 7.0 %copy-start.10 = (bf16[256,256]{1,0:T(8,128)(2,1)S(1)}, bf16[256,256]{1,0:T(8,128)(2,1)}, u32[]{:S(2)}) copy-start(bf16[256,256]{1,0:T(8,128)(2,1)} %copy-done.9) | copy-start | bytes 393220
  63.1 12.3 %collective-permute-start.14 = (bf16[256,640]{1,0:T(8,128)(2,1)}, bf16[256,640]{1,0:T(8,128)(2,1)S(1)}, u32[]{:S(2)}, u32[]{:S(2)}) collective-permute-start(bf16[256,640]{1,0:T(8,128)(2,1)} %get-tuple-element.100.refs_0_), channel_id=1, source_target_pairs={{0,1},{1,0},{2,3},{3,2},{4,5},{5,4},{6,7},{7,6},{8,9},{9,8},{10,11... | collective-permute-start | bytes 983048 | tf_op jit(solution)/shard_map/ppermute | solution.py:62
  69.9 12.4 %collective-permute-start.16 = (bf16[256,640]{1,0:T(8,128)(2,1)}, bf16[256,640]{1,0:T(8,128)(2,1)S(1)}, u32[]{:S(2)}, u32[]{:S(2)}) collective-permute-start(bf16[256,640]{1,0:T(8,128)(2,1)} %get-tuple-element.100.refs_0_), channel_id=1, source_target_pairs={{0,2},{2,0},{1,3},{3,1},{4,6},{6,4},{5,7},{7,5},{8,10},{10,8},{9,1... | collective-permute-start | bytes 983048 | tf_op jit(solution)/shard_map/ppermute | solution.py:62
  74.0 1.4 %collective-permute-start.15 = (bf16[256,256]{1,0:T(8,128)(2,1)S(1)}, bf16[256,256]{1,0:T(8,128)(2,1)S(1)}, u32[]{:S(2)}, u32[]{:S(2)}) collective-permute-start(bf16[256,256]{1,0:T(8,128)(2,1)S(1)} %last.3.refs_1_), channel_id=1, source_target_pairs={{0,1},{1,0},{2,3},{3,2},{4,5},{5,4},{6,7},{7,6},{8,9},{9,8},{10,11... | collective-permute-start | bytes 393224 | tf_op jit(solution)/shard_map/ppermute | solution.py:62
  74.4 7.8 %collective-permute-start.17 = (bf16[256,256]{1,0:T(8,128)(2,1)S(1)}, bf16[256,256]{1,0:T(8,128)(2,1)S(1)}, u32[]{:S(2)}, u32[]{:S(2)}) collective-permute-start(bf16[256,256]{1,0:T(8,128)(2,1)S(1)} %last.3.refs_1_), channel_id=1, source_target_pairs={{0,2},{2,0},{1,3},{3,1},{4,6},{6,4},{5,7},{7,5},{8,10},{10,8},{9,1... | collective-permute-start | bytes 393224 | tf_op jit(solution)/shard_map/ppermute | solution.py:62
  75.5 2.8 %copy-start = (bf16[3584,896]{1,0:T(8,128)(2,1)S(1)}, bf16[3584,896]{1,0:T(8,128)(2,1)}, u32[]{:S(2)}) copy-start(bf16[3584,896]{1,0:T(8,128)(2,1)} %weight.1) | copy-start | bytes 19267588
  82.2 2.2 %collective-permute-start.18 = (bf16[256,640]{1,0:T(8,128)(2,1)S(1)}, bf16[256,640]{1,0:T(8,128)(2,1)S(1)}, u32[]{:S(2)}, u32[]{:S(2)}) collective-permute-start(bf16[256,640]{1,0:T(8,128)(2,1)S(1)} %collective-permute-done.16.refs_0_), channel_id=1, source_target_pairs={{0,1},{1,0},{2,3},{3,2},{4,5},{5,4},{6,7},{7,6},{8,9},{9,8},{10,11... | collective-permute-start | bytes 983048 | tf_op jit(solution)/shard_map/ppermute | solution.py:62
  83.0 1.4 %collective-permute-start.19 = (bf16[256,256]{1,0:T(8,128)(2,1)S(1)}, bf16[256,256]{1,0:T(8,128)(2,1)S(1)}, u32[]{:S(2)}, u32[]{:S(2)}) collective-permute-start(bf16[256,256]{1,0:T(8,128)(2,1)S(1)} %collective-permute-done.17.refs_2_), channel_id=1, source_target_pairs={{0,1},{1,0},{2,3},{3,2},{4,5},{5,4},{6,7},{7,6},{8,9},{9,8},{10,11... | collective-permute-start | bytes 393224 | tf_op jit(solution)/shard_map/ppermute | solution.py:62
